TPU v7x, 32 devices: a whole 2x2x4 slice. The times are simulated.
32 devices in a mesh: chan: 8 (over z, x), tile: 4 (over y, core).
Axes of the slice: x: 2, y: 2, z: 4, core: 2. Of those that a mesh axis runs over, the one named last changes fastest.
Arguments:
- voltage: float32 [2, 64, 512, 1024], P(None, 'tile', 'chan'), may hold values from -6 to 6
- fir_taps: float32 [4, 1024], replicated, may hold values from -3 to 3
- tile_slot: int32 [10], replicated, may hold values from 0 to 11, as said below
- tile_blocks: int32 [10, 2], replicated, may hold values from 0 to 3, as said below
Outputs:
- visibility: float32 [12, 1024, 2, 128, 128], P('tile', 'chan')
Inputs may be any that keep to these rules, and one draw needn't show every extreme that they name: `tile_slot`: the values are distinct; slot g belongs to device g // 3 of the tile axis. Every device of the tile axis holds at least one tile and at most 3, some exactly 3, and a device's tiles fill its lowest slots. `tile_blocks`: the unordered pairs of the rows are the 10 pairs of blocks p <= q, each once; a row may name its pair in either order.
All inputs are finite; a program needn't handle non-finite values.
Results may differ from a plain program's by a relative error of at most 0.0001.
Values sent between devices are 32-bit elements; how exact they have to be, the bound alone decides.
No kernel may reach another device: no remote copies, remote signals or barrier semaphores. Data moves between devices by JAX's collectives and lax.ppermute only.
A program may use at most 256 MiB of HBM per device.

v0:
```python
import functools
import math

import jax
import jax.numpy as jnp
import numpy as np
from jax import lax
from jax.experimental import pallas as pl
from jax.experimental.pallas import tpu as pltpu
from jax.sharding import PartitionSpec as P

BLOCK = 128
RADIX = 4
STEP = 256
VMEM_BYTES = 20 * 1024 * 1024
BF16 = jnp.bfloat16
F32 = jnp.float32


def shifted(value, axis, steps):
    count = lax.axis_size(axis)
    initial, last = (max(0, -steps), min(count, count - steps))
    return lax.ppermute(value, axis, [(source, source + steps) for source in range(initial, last)])


def swapped(value, axis, mask):
    count = lax.axis_size(axis)
    return lax.ppermute(value, axis, [(source, source ^ mask) for source in range(count)])


def params():
    return pltpu.CompilerParams(vmem_limit_bytes=VMEM_BYTES)


def split(value):
    high = value.astype(BF16)
    return high, (value - high.astype(F32)).astype(BF16)


def filter_frames(voltage, fir_taps):
    tap_count = fir_taps.shape[0]
    frames = voltage.shape[1]
    history = shifted(voltage[:, : tap_count - 1], "tile", -1)
    extended = jnp.concatenate([voltage, history], axis=1)
    filtered = jnp.zeros(voltage.shape, jnp.float32)
    for tap_index in range(tap_count):
        filtered = (
            filtered
            + fir_taps[tap_index][None, None, None, :] * extended[:, tap_index : tap_index + frames]
        )
    return filtered


def transform(filtered):
    channel_count = filtered.shape[3]
    row_count = filtered.shape[1] * filtered.shape[2]
    position = lax.broadcasted_iota(jnp.int32, (channel_count, channel_count), 0)
    frequency = lax.broadcasted_iota(jnp.int32, (channel_count, channel_count), 1)
    phase_angle = (position * frequency % channel_count).astype(jnp.float32) * (
        2.0 * math.pi / channel_count
    )
    factor = 1.0 / math.sqrt(channel_count)
    cosine = jnp.cos(phase_angle) * factor
    sine_table = jnp.sin(phase_angle) * factor
    samples = filtered.reshape(2 * row_count, channel_count)
    cos_part = jnp.dot(
        cosine, samples.T, precision=lax.Precision.HIGHEST, preferred_element_type=jnp.float32
    )
    sin_part = jnp.dot(
        sine_table, samples.T, precision=lax.Precision.HIGHEST, preferred_element_type=jnp.float32
    )
    real_part = cos_part[:, :row_count] + sin_part[:, row_count:]
    imag_part = cos_part[:, row_count:] - sin_part[:, :row_count]
    joined = jnp.concatenate([real_part, imag_part], axis=1)
    return joined.reshape(channel_count, 2, filtered.shape[1], filtered.shape[2])


def tile_product(gathered, row_block, col_block, block_width):
    left_block = lax.dynamic_slice_in_dim(gathered, row_block * block_width, block_width, 3)
    right_block = lax.dynamic_slice_in_dim(gathered, col_block * block_width, block_width, 3)
    channel_count = gathered.shape[0]
    depth = 2 * gathered.shape[2]
    left_real = left_block.reshape(channel_count, depth, block_width)
    left_imag = jnp.concatenate([left_block[:, 1], -left_block[:, 0]], axis=1)
    left_both = jnp.concatenate([left_real, left_imag], axis=2)
    right_both = right_block.reshape(channel_count, depth, block_width)
    return jnp.einsum(
        "cki,ckj->cij",
        left_both,
        right_both,
        precision=lax.Precision.HIGHEST,
        preferred_element_type=jnp.float32,
    )


def own_slots(tile_slot, tile_blocks, slot_count):
    first_slot = lax.axis_index("tile") * slot_count
    row_blocks = []
    col_blocks = []
    present = []
    for slot_index in range(slot_count):
        matches = (tile_slot == first_slot + slot_index).astype(jnp.int32)
        row_blocks.append(jnp.sum(matches * tile_blocks[:, 0]))
        col_blocks.append(jnp.sum(matches * tile_blocks[:, 1]))
        present.append(jnp.sum(matches))
    return row_blocks, col_blocks, present


def generic_body(voltage, fir_taps, tile_slot, tile_blocks):
    spectra = transform(filter_frames(voltage, fir_taps))
    tile_count = tile_blocks.shape[0]
    tile_size = lax.axis_size("tile")
    slot_count = (tile_count + tile_size - 1) // tile_size
    turned = lax.all_to_all(spectra, "chan", split_axis=0, concat_axis=3, tiled=True)
    spectra_total = turned.shape[2] * tile_size
    row_blocks, col_blocks, present = own_slots(tile_slot, tile_blocks, slot_count)
    portion = lax.all_gather(turned, "tile", axis=2, tiled=True)
    summed = jnp.stack(
        [
            tile_product(portion, row_blocks[slot_index], col_blocks[slot_index], BLOCK)
            for slot_index in range(slot_count)
        ]
    )
    weights = jnp.stack(present).astype(F32)[:, None, None, None] / spectra_total
    return (summed * weights).reshape(slot_count, turned.shape[0], 2, BLOCK, BLOCK)


def fourier_table(points, owners, scale):
    phase = np.outer(np.arange(points), np.arange(points)) % points
    angle = phase * (2.0 * math.pi / points)
    cosine = np.cos(angle) * scale
    sine = np.sin(angle) * scale
    both = np.stack([np.concatenate([cosine, sine], 1), np.concatenate([-sine, cosine], 1)], 0)
    both = both.reshape(2, owners, points // owners, 2 * points).transpose(1, 0, 2, 3)
    return both.reshape(owners, -1, 2 * points).astype(np.float32)


def twiddle_table(length):
    angle = np.outer(np.arange(1, RADIX), np.arange(length // RADIX)) * (2.0 * math.pi / length)
    return np.stack([np.cos(angle), np.sin(angle)], 1).reshape(-1, length // RADIX).astype(np.float32)


def filter_kernel(frames, voltage_ref, next_ref, taps_ref, twiddle_ref, *refs):
    out_refs = refs[-2 * RADIX :]
    tap_count, length = taps_ref.shape
    held = voltage_ref.shape[1]
    points = length // RADIX

    def quarter(part, frame, index):
        lanes = slice(index * points, (index + 1) * points)
        total = None
        for tap in range(tap_count):
            at = frame + tap
            source = voltage_ref[part, at, :, lanes] if at < held else next_ref[part, at - held, :, lanes]
            term = source * taps_ref[pl.ds(tap, 1), lanes]
            total = term if total is None else total + term
        return total

    for frame in range(frames):
        real = [quarter(0, frame, index) for index in range(RADIX)]
        imag = [quarter(1, frame, index) for index in range(RADIX)]
        even_real, odd_real = real[0] + real[2], real[1] + real[3]
        even_imag, odd_imag = imag[0] + imag[2], imag[1] + imag[3]
        left_real, right_real = real[0] - real[2], real[1] - real[3]
        left_imag, right_imag = imag[0] - imag[2], imag[1] - imag[3]
        residues = [
            (even_real + odd_real, even_imag + odd_imag),
            (left_real + right_imag, left_imag - right_real),
            (even_real - odd_real, even_imag - odd_imag),
            (left_real - right_imag, left_imag + right_real),
        ]
        for index, (re, im) in enumerate(residues):
            if index:
                cosine = twiddle_ref[pl.ds(2 * index - 2, 1), :]
                sine = twiddle_ref[pl.ds(2 * index - 1, 1), :]
                re, im = re * cosine + im * sine, im * cosine - re * sine
            for part, value in enumerate((re, im)):
                high, low = split(value)
                lanes = slice(part * points, (part + 1) * points)
                out_refs[2 * index][frame, :, lanes] = high
                out_refs[2 * index + 1][frame, :, lanes] = low


def filtered_samples(voltage, following, fir_taps, late, earlier, after):
    _, frames, inputs, length = voltage.shape
    width = 16
    depth = 2 * length // RADIX
    twiddles = jnp.asarray(twiddle_table(length))
    out = jax.ShapeDtypeStruct((frames, inputs, depth), BF16)
    if earlier:
        count, held, place = late, late, frames // late - 1
    else:
        count, held, place = frames - late, frames, 0
    others = list(earlier) + list(after)
    return pl.pallas_call(
        functools.partial(filter_kernel, count),
        grid=(inputs // width,),
        in_specs=[
            pl.BlockSpec((2, held, width, length), lambda i: (0, place, i, 0)),
            pl.BlockSpec((2, following.shape[1], width, length), lambda i: (0, 0, i, 0)),
            pl.BlockSpec(fir_taps.shape, lambda i: (0, 0)),
            pl.BlockSpec(twiddles.shape, lambda i: (0, 0)),
        ]
        + [pl.BlockSpec(memory_space=pl.ANY)] * len(others),
        out_specs=[pl.BlockSpec((count, width, depth), lambda i: (place, i, 0))] * (2 * RADIX),
        out_shape=[out] * (2 * RADIX),
        input_output_aliases={4 + index: index for index in range(len(earlier))},
        compiler_params=params(),
        cost_estimate=pl.CostEstimate(
            flops=16 * voltage.size * count // frames,
            bytes_accessed=8 * voltage.size * count // frames,
            transcendentals=0,
        ),
        name="filter",
    )(voltage, following, fir_taps, twiddles, *others)


def dot_rows(left, right):
    return lax.dot_general(left, right, (((1,), (1,)), ((), ())), preferred_element_type=F32)


def transform_kernel(groups, pieces, table_ref, xh_ref, xl_ref, *refs):
    out_refs, (th_ref, tl_ref) = refs[-2 - len(groups) * pieces : -2], refs[-2:]
    height = table_ref.shape[1]
    masks = [mask for group in groups for mask in group]

    @pl.when(pl.program_id(0) == 0)
    def _():
        me = lax.axis_index("chan")
        for index, mask in enumerate(masks):
            rows = slice(index * height, (index + 1) * height)
            th_ref[rows], tl_ref[rows] = split(table_ref[me ^ mask])

    high = xh_ref[...]
    result = dot_rows(th_ref[...], high) + dot_rows(th_ref[...], xl_ref[...])
    result = result + dot_rows(tl_ref[...], high)
    count = height // 2
    size = count // pieces
    places = [(which, at) for which, group in enumerate(groups) for at in range(len(group))]
    for index, (which, at) in enumerate(places):
        for part in range(2):
            for piece in range(pieces):
                first = index * height + part * count + piece * size
                for column in range(result.shape[1] // BLOCK):
                    out_refs[which * pieces + piece][at, part, column] = result[
                        first : first + size, column * BLOCK : (column + 1) * BLOCK
                    ]


def transformed(groups, pieces, table, samples, after, first, last):
    depth = samples[0].shape[1]
    owners, height, _ = table.shape
    size = height // 2 // pieces
    step = STEP
    rows = (last - first) * step
    row_spec = pl.BlockSpec((step, depth), lambda i: (first + i, 0))
    total = sum(map(len, groups)) * height
    counts = [len(group) for group in groups for _ in range(pieces)]
    return pl.pallas_call(
        functools.partial(transform_kernel, groups, pieces),
        grid=(rows // step,),
        in_specs=[pl.BlockSpec(table.shape, lambda i: (0, 0, 0)), row_spec, row_spec]
        + [pl.BlockSpec(memory_space=pl.ANY)] * len(after),
        out_specs=[
            pl.BlockSpec((count, 2, step // BLOCK, size, BLOCK), lambda i: (0, 0, i, 0, 0))
            for count in counts
        ],
        out_shape=[
            jax.ShapeDtypeStruct((count, 2, rows // BLOCK, size, BLOCK), F32) for count in counts
        ],
        scratch_shapes=[pltpu.VMEM((total, depth), BF16)] * 2,
        compiler_params=params(),
        cost_estimate=pl.CostEstimate(
            flops=3 * 2 * total * depth * rows,
            bytes_accessed=4 * depth * rows + 4 * table.size + 4 * total * rows,
            transcendentals=0,
        ),
        name="transform",
    )(table, *samples, *after)


def merge_kernel(count, groups, piece, *refs):
    near_refs, far_refs, out_refs = refs[: len(groups)], refs[len(groups) : 2 * len(groups)], refs[-count:]
    total = sum(groups)
    odd = lax.axis_index("chan") % 2 == 1
    lower = lax.broadcasted_iota(jnp.int32, (total, BLOCK), 1) < BLOCK // 2
    for unit, out_ref in enumerate(out_refs):
        for channel in range(piece):
            for part in range(2):

                def rows_of(segment_refs):
                    rows = [
                        ref[pl.ds((unit * 2 + part) * held * piece + channel, held, stride=piece), :]
                        for ref, held in zip(segment_refs, groups)
                    ]
                    return rows[0] if len(rows) == 1 else jnp.concatenate(rows, axis=0)

                near, far = rows_of(near_refs), rows_of(far_refs)
                first = jnp.where(odd, far, near)
                second = jnp.where(odd, near, far)
                at = part * 2 * total
                out_ref[channel, at : at + total] = jnp.where(
                    lower, first, pltpu.roll(second, BLOCK // 2, 1)
                )
                out_ref[channel, at + total : at + 2 * total] = jnp.where(
                    lower, pltpu.roll(first, BLOCK // 2, 1), second
                )


def merged(near, far, after):
    count, _, _, piece, lanes = near[0].shape
    groups = [value.shape[2] for value in near]
    size = sum(value.size for value in near)
    return pl.pallas_call(
        functools.partial(merge_kernel, count, groups, piece),
        in_specs=[pl.BlockSpec(memory_space=pltpu.VMEM)] * (2 * len(near))
        + [pl.BlockSpec(memory_space=pl.ANY)] * len(after),
        out_specs=[pl.BlockSpec(memory_space=pltpu.VMEM)] * count,
        out_shape=[jax.ShapeDtypeStruct((piece, 4 * sum(groups), lanes), F32)] * count,
        compiler_params=params(),
        cost_estimate=pl.CostEstimate(flops=4 * size, bytes_accessed=16 * size, transcendentals=0),
        name="merge",
    )(*[value.reshape(-1, lanes) for value in list(near) + list(far)], *after)


def pack_kernel(counts, *refs):
    sources = iter(refs)
    for count, out_ref in zip(counts, refs[-len(counts) :]):
        for index in range(count):
            out_ref[index] = next(sources)[...]


def packed(batches, after):
    counts = [len(batch) for batch in batches]
    values = [value for batch in batches for value in batch]
    width = 8

    def spec(shape):
        lead = shape[:-3]
        return pl.BlockSpec(
            lead + (min(width, shape[-3]),) + shape[-2:], lambda i: (0,) * len(lead) + (i, 0, 0)
        )

    shapes = [(len(batch),) + batch[0].shape for batch in batches]
    return pl.pallas_call(
        functools.partial(pack_kernel, counts),
        grid=(values[0].shape[-3] // min(width, values[0].shape[-3]),),
        in_specs=[spec(value.shape) for value in values]
        + [pl.BlockSpec(memory_space=pl.ANY)] * len(after),
        out_specs=[spec(shape) for shape in shapes],
        out_shape=[jax.ShapeDtypeStruct(shape, F32) for shape in shapes],
        compiler_params=params(),
        cost_estimate=pl.CostEstimate(
            flops=0, bytes_accessed=8 * sum(value.size for value in values), transcendentals=0
        ),
        name="pack",
    )(*values, *after)


def dot_columns(left, right):
    return lax.dot_general(left, right, (((0,), (0,)), ((), ())), preferred_element_type=F32)


def correlate_kernel(slots, tiles, order, slot_ref, blocks_ref, *refs):
    unit_refs = []
    for ref in refs[:-5]:
        if len(ref.shape) == 4:
            unit_refs.append(ref)
        elif len(ref.shape) == 5 and len(unit_refs) < tiles:
            unit_refs += [ref.at[0], ref.at[1]]
    out_ref, done_ref, high_ref, low_ref, place_ref = refs[-5:]
    done_ref[...] = jnp.zeros(done_ref.shape, F32)
    blocks, width, depth, _ = unit_refs[0].shape
    rows = depth // 2
    half = tiles * rows

    @pl.when(pl.program_id(0) == 0)
    def _():
        first_slot = lax.axis_index("tile") * slots
        for slot in range(slots):
            row = jnp.int32(0)
            col = jnp.int32(0)
            present = jnp.int32(0)
            for tile in range(slot_ref.shape[0]):
                match = (slot_ref[tile] == first_slot + slot).astype(jnp.int32)
                row = row + match * blocks_ref[2 * tile]
                col = col + match * blocks_ref[2 * tile + 1]
                present = present + match
            place_ref[3 * slot] = row
            place_ref[3 * slot + 1] = col
            place_ref[3 * slot + 2] = present

    own = lax.axis_index("chan") // 2
    for channel in range(width):
        for mask in range(blocks):
            block = own ^ order[mask]
            for part in range(2):
                joined = jnp.concatenate(
                    [
                        unit_ref[mask, channel, part * rows : (part + 1) * rows]
                        for unit_ref in unit_refs
                    ],
                    axis=0,
                )
                high, low = split(joined)
                high_ref[channel, block, part * half : (part + 1) * half] = high
                low_ref[channel, block, part * half : (part + 1) * half] = low
        for slot in range(slots):
            row = place_ref[3 * slot]
            col = place_ref[3 * slot + 1]
            weight = place_ref[3 * slot + 2].astype(F32)
            row_high = high_ref[channel, row]
            row_low = low_ref[channel, row]
            col_high = high_ref[channel, col]
            col_low = low_ref[channel, col]
            turned_high = jnp.concatenate([-col_high[half:], col_high[:half]], axis=0)
            turned_low = jnp.concatenate([-col_low[half:], col_low[:half]], axis=0)
            right_high = jnp.concatenate([col_high, turned_high], axis=1)
            right_low = jnp.concatenate([col_low, turned_low], axis=1)
            value = dot_columns(
                jnp.concatenate([row_high, row_low], axis=0),
                jnp.concatenate([right_high, right_high], axis=0),
            ) + dot_columns(row_high, right_low)
            value = value * weight
            out_ref[slot, channel, 0] = value[:, :BLOCK]
            out_ref[slot, channel, 1] = value[:, BLOCK:]


def correlated(order, tile_slot, tile_blocks, units, visibility, residue, first, total, slots):
    tiles = sum(1 if unit.ndim == 4 else unit.shape[0] for unit in units)
    blocks, piece, depth, lanes = units[0].shape
    width = 4
    out = jax.ShapeDtypeStruct((slots, total, RADIX, 2, BLOCK, BLOCK), F32)
    operands = [tile_slot, tile_blocks.reshape(-1)] + units
    in_specs = [
        pl.BlockSpec((blocks, width, depth, lanes), lambda i, *_: (0, i, 0, 0))
        if unit.ndim == 4
        else pl.BlockSpec(unit.shape[:2] + (width, depth, lanes), lambda i, *_: (0, 0, i, 0, 0))
        for unit in units
    ]
    aliases = {}
    if visibility is not None:
        operands.append(visibility)
        in_specs.append(pl.BlockSpec(memory_space=pl.ANY))
        aliases = {len(operands) - 1: 0}
    return pl.pallas_call(
        functools.partial(correlate_kernel, slots, tiles, order),
        grid_spec=pltpu.PrefetchScalarGridSpec(
            num_scalar_prefetch=2,
            grid=(piece // width,),
            in_specs=in_specs,
            out_specs=[
                pl.BlockSpec(
                    (slots, width, None, 2, BLOCK, BLOCK), lambda i, *_: (0, first // width + i, residue, 0, 0, 0)
                ),
                pl.BlockSpec((8, BLOCK), lambda i, *_: (0, 0)),
            ],
            scratch_shapes=[pltpu.VMEM((width, blocks, tiles * depth, lanes), BF16)] * 2
            + [pltpu.SMEM((3 * slots,), jnp.int32)],
        ),
        out_shape=[out, jax.ShapeDtypeStruct((8, BLOCK), F32)],
        input_output_aliases=aliases,
        compiler_params=params(),
        cost_estimate=pl.CostEstimate(
            flops=3 * 2 * slots * piece * tiles * depth * BLOCK * 2 * BLOCK,
            bytes_accessed=4 * piece * lanes * (tiles * blocks * depth + slots * 2 * BLOCK),
            transcendentals=0,
        ),
        name="correlate",
    )(*operands)


def body(voltage, fir_taps, tile_slot, tile_blocks):
    _, frames, inputs, length = voltage.shape
    tap_count = fir_taps.shape[0]
    owners = lax.axis_size("chan")
    tiles = lax.axis_size("tile")
    channels = length // owners
    blocks = owners // 2
    slots = -(-tile_blocks.shape[0] // tiles)
    scale = 1.0 / math.sqrt(length * frames * tiles)
    table = jnp.asarray(fourier_table(length // RADIX, owners, scale))

    order = list(range(2, blocks)) + [1, 0]
    groups = [tuple(2 * block + x for block in order) for x in range(2)]
    halves = 2
    size = channels // RADIX // halves
    count = RADIX * halves
    near = [[] for _ in range(count)]
    share = [[] for _ in range(count)]
    away = [None] * count
    units = [None] * count
    paired = [None] * count

    steps = frames * inputs // STEP
    late = STEP // inputs
    following = shifted(voltage[:, : tap_count - 1], "tile", -1)
    early = filtered_samples(voltage, voltage[:, : tap_count - 1], fir_taps, late, [], [])

    def spectra(samples, residue, after, first, last):
        rows = [value.reshape(frames * inputs, -1) for value in samples[2 * residue : 2 * residue + 2]]
        values = transformed(groups, halves, table, rows, after, first, last)
        for half in range(halves):
            near[residue * halves + half].append(values[half])
            share[residue * halves + half].append(values[halves + half])

    spectra(early, 0, [], 0, steps - 1)
    samples = filtered_samples(voltage, following, fir_taps, late, early, [near[0][0]])
    spectra(samples, 0, [], steps - 1, steps)
    spectra(samples, 1, [], 0, steps)

    def leave(piece):
        values = share[piece]
        if 0 < piece < 4:
            after = [away[piece - 1][-1]]
            values = [packed([[value]], after)[0].reshape(value.shape) for value in values]
        away[piece] = [swapped(value, "chan", 1) for value in values]

    def merge(piece, after):
        units[piece] = merged(near[piece], away[piece], after)

    def along(piece):
        return [
            swapped(unit, "chan", 2 * block) if block else unit
            for block, unit in zip(order, units[piece])
        ]

    leave(0)
    merge(0, near[halves][:1])
    turned = along(0)
    for residue in range(2, RADIX):
        spectra(samples, residue, turned[-2:-1], 0, steps)
    leave(1)
    merge(1, [])
    leave(2)

    def products(piece, arrays, visibility):
        return correlated(
            order, tile_slot, tile_blocks, arrays, visibility,
            piece // halves, piece % halves * size, channels // RADIX, slots,
        )

    visibility = None
    finished = []
    pair = None
    for piece in range(count):
        if piece:
            after = [pair[1]]
            for later in range(piece + 1, min(piece + 3, count)):
                if units[later] is None:
                    merge(later, [])
                after.append(units[later][0])
        else:
            after = [units[1][0]] + [near[residue * halves][0] for residue in range(2, RADIX)]
        after += finished[piece - 2 : piece - 1] if piece >= 2 else []
        (own,) = packed([turned], after)
        if piece + 1 < count:
            turned = along(piece + 1)
        across = swapped(own, "tile", 2)
        if piece + 3 < count:
            leave(piece + 3)
        if pair:
            (both,) = packed([pair], [own] + (away[piece + 3][-1:] if piece + 3 < count else []))
            paired[piece - 1] = swapped(both, "tile", 1)
            visibility, token = products(piece - 1, pair + [paired[piece - 1]], visibility)
            finished.append(token)
        pair = [own, across]
    (last,) = packed([[across]], finished[-1:])
    arrays = pair + [swapped(own, "tile", 1), swapped(last[0], "tile", 1)]
    visibility, _ = products(count - 1, arrays, visibility)
    return visibility.reshape(slots, channels, 2, BLOCK, BLOCK)


def solution(mesh):
    in_specs = (P(None, "tile", "chan", None), P(), P(), P())
    out_specs = P("tile", "chan", None, None, None)
    owners, tiles = mesh.shape["chan"], mesh.shape["tile"]

    def run(voltage, fir_taps, tile_slot, tile_blocks):
        paired = 2 * voltage.shape[2] == BLOCK * owners and tiles == 4
        chosen = body if paired else generic_body
        return jax.shard_map(
            chosen, mesh=mesh, in_specs=in_specs, out_specs=out_specs, check_vma=False
        )(voltage, fir_taps, tile_slot, tile_blocks)

    return run
```

profile of v0, /device:TPU:13, one launch (start us, length us, event | category | flops | bytes accessed | tf_op | source)
XLA Modules:
  0.0 282.1 jit_solution(4708533309790630310)
XLA Ops:
  7.6 4.3 %filter.2 = (bf16[16,64,512]{2,1,0:T(8,128)(2,1)S(1)}, bf16[16,64,512]{2,1,0:T(8,128)(2,1)S(1)}, bf16[16,64,512]{2,1,0:T(8,128)(2,1)S(1)}, bf16[16,64,512]{2,1,0...) custom-call(f32[2,16,64,1024]{3,2,1,0:T(8,128)S(1)} %copy-done, ...), custom_call_target="tpu_custom_call" | custom-call | flops 25165824 | bytes 12582912 | tf_op jit(solution)/shard_map/filter/pallas_call | solution.py:195
  20.6 4.3 %collective-permute-done.1 = f32[4,2,6,16,128]{4,3,2,1,0:T(8,128)S(1)} collective-permute-done((f32[4,2,6,16,128]{4,3,2,1,0:T(8,128)S(1)}, f32[4,2,6,16,128]{4,3,2,1,0:T(8,128)S(1)}, u32[]{:S(2)}, u32[]{:S(2)}) %collective-permute-start.1) | collective-permute-done | bytes 393248 | tf_op jit(solution)/shard_map/ppermute | solution.py:28
  41.5 11.1 %collective-permute-done.34.refs_1_ = f32[16,32,128]{2,1,0:T(8,128)S(1)} collective-permute-done((f32[16,32,128]{2,1,0:T(8,128)S(1)}, f32[16,32,128]{2,1,0:T(8,128)S(1)}, u32[]{:S(2)}, u32[]{:S(2)}) %collective-permute-start.34) | collective-permute-done | bytes 262176 | tf_op jit(solution)/shard_map/ppermute | solution.py:28
  59.8 10.8 %collective-permute-done.22 = f32[4,2,8,16,128]{4,3,2,1,0:T(8,128)S(1)} collective-permute-done((f32[4,2,8,16,128]{4,3,2,1,0:T(8,128)S(1)}, f32[4,2,8,16,128]{4,3,2,1,0:T(8,128)S(1)}, u32[]{:S(2)}, u32[]{:S(2)}) %collective-permute-start.22) | collective-permute-done | bytes 524320 | tf_op jit(solution)/shard_map/ppermute | solution.py:28
  75.3 8.0 %collective-permute-done.31.refs_1_ = f32[16,32,128]{2,1,0:T(8,128)S(1)} collective-permute-done((f32[16,32,128]{2,1,0:T(8,128)S(1)}, f32[16,32,128]{2,1,0:T(8,128)S(1)}, u32[]{:S(2)}, u32[]{:S(2)}) %collective-permute-start.31) | collective-permute-done | bytes 262176 | tf_op jit(solution)/shard_map/ppermute | solution.py:28
  96.8 5.3 %correlate.8 = (f32[3,32,4,2,128,128]{5,4,3,2,1,0:T(8,128)}, f32[8,128]{1,0:T(8,128)S(1)}) custom-call(s32[10]{0:T(128)S(1)} %copy-done.21, s32[20]{0:T(128)S(1)} %reshape.115.blocks_ref, f32[4,16,32,128]{3,2,1,0:T(8,128)S(1)} %copy-done.3, f32[4,16,32,128]{3,2,1,0:T(8,128)S(1)} %collective-permute-done.35.refs_4_.refs_1_, f32[2,4,16,32,128]{4,3,2,1,0:T(8,128)S(1)} %copy-done.23), custom_call_target="tpu_custom_call" | custom-call | flops 1207959552 | bytes 10485760 | tf_op jit(solution)/shard_map/correlate/pallas_call | solution.py:446
  104.8 7.7 %collective-permute-done.27.refs_1_ = f32[16,32,128]{2,1,0:T(8,128)} collective-permute-done((f32[16,32,128]{2,1,0:T(8,128)}, f32[16,32,128]{2,1,0:T(8,128)}, u32[]{:S(2)}, u32[]{:S(2)}) %collective-permute-start.27) | collective-permute-done | bytes 262176 | tf_op jit(solution)/shard_map/ppermute | solution.py:28
  121.7 5.3 %correlate.9 = (f32[3,32,4,2,128,128]{5,4,3,2,1,0:T(8,128)}, f32[8,128]{1,0:T(8,128)S(1)}) custom-call(s32[10]{0:T(128)S(1)} %copy-done.21, s32[20]{0:T(128)S(1)} %reshape.115.blocks_ref, f32[4,16,32,128]{3,2,1,0:T(8,128)S(1)} %pack.25.refs_2_.refs_0_, ...), custom_call_target="tpu_custom_call", output_to_operand_aliasing={{0}: (5, {})} | custom-call | flops 1207959552 | bytes 10485760 | tf_op jit(solution)/shard_map/correlate/pallas_call | solution.py:446
  127.0 6.3 %collective-permute-done.23.refs_0_ = f32[16,32,128]{2,1,0:T(8,128)S(1)} collective-permute-done((f32[16,32,128]{2,1,0:T(8,128)S(1)}, f32[16,32,128]{2,1,0:T(8,128)S(1)}, u32[]{:S(2)}, u32[]{:S(2)}) %collective-permute-start.23) | collective-permute-done | bytes 262176 | tf_op jit(solution)/shard_map/ppermute | solution.py:28
  133.3 6.5 %collective-permute-done.24.refs_1_ = f32[16,32,128]{2,1,0:T(8,128)S(1)} collective-permute-done((f32[16,32,128]{2,1,0:T(8,128)S(1)}, f32[16,32,128]{2,1,0:T(8,128)S(1)}, u32[]{:S(2)}, u32[]{:S(2)}) %collective-permute-start.24) | collective-permute-done | bytes 262176 | tf_op jit(solution)/shard_map/ppermute | solution.py:28
  147.2 5.3 %correlate.10 = (f32[3,32,4,2,128,128]{5,4,3,2,1,0:T(8,128)}, f32[8,128]{1,0:T(8,128)S(1)}) custom-call(s32[10]{0:T(128)S(1)} %copy-done.21, s32[20]{0:T(128)S(1)} %reshape.115.blocks_ref, f32[4,16,32,128]{3,2,1,0:T(8,128)S(1)} %pack.27.refs_2_.refs_0_, ...), custom_call_target="tpu_custom_call", output_to_operand_aliasing={{0}: (5, {})} | custom-call | flops 1207959552 | bytes 10485760 | tf_op jit(solution)/shard_map/correlate/pallas_call | solution.py:446
  152.5 7.4 %collective-permute-done.17.refs_0_ = f32[16,32,128]{2,1,0:T(8,128)S(1)} collective-permute-done((f32[16,32,128]{2,1,0:T(8,128)S(1)}, f32[16,32,128]{2,1,0:T(8,128)S(1)}, u32[]{:S(2)}, u32[]{:S(2)}) %collective-permute-start.17) | collective-permute-done | bytes 262176 | tf_op jit(solution)/shard_map/ppermute | solution.py:28
  159.8 7.7 %collective-permute-done.18.refs_1_ = f32[16,32,128]{2,1,0:T(8,128)S(1)} collective-permute-done((f32[16,32,128]{2,1,0:T(8,128)S(1)}, f32[16,32,128]{2,1,0:T(8,128)S(1)}, u32[]{:S(2)}, u32[]{:S(2)}) %collective-permute-start.18) | collective-permute-done | bytes 262176 | tf_op jit(solution)/shard_map/ppermute | solution.py:28
  174.9 5.3 %correlate.11 = (f32[3,32,4,2,128,128]{5,4,3,2,1,0:T(8,128)}, f32[8,128]{1,0:T(8,128)S(1)}) custom-call(s32[10]{0:T(128)S(1)} %copy-done.21, s32[20]{0:T(128)S(1)} %reshape.115.blocks_ref, f32[4,16,32,128]{3,2,1,0:T(8,128)S(1)} %pack.29.refs_2_.refs_0_, ...), custom_call_target="tpu_custom_call", output_to_operand_aliasing={{0}: (5, {})} | custom-call | flops 1207959552 | bytes 10485760 | tf_op jit(solution)/shard_map/correlate/pallas_call | solution.py:446
  180.2 7.7 %collective-permute-done.13.refs_0_ = f32[16,32,128]{2,1,0:T(8,128)S(1)} collective-permute-done((f32[16,32,128]{2,1,0:T(8,128)S(1)}, f32[16,32,128]{2,1,0:T(8,128)S(1)}, u32[]{:S(2)}, u32[]{:S(2)}) %collective-permute-start.13) | collective-permute-done | bytes 262176 | tf_op jit(solution)/shard_map/ppermute | solution.py:28
  187.9 6.5 %collective-permute-done.14.refs_1_ = f32[16,32,128]{2,1,0:T(8,128)S(1)} collective-permute-done((f32[16,32,128]{2,1,0:T(8,128)S(1)}, f32[16,32,128]{2,1,0:T(8,128)S(1)}, u32[]{:S(2)}, u32[]{:S(2)}) %collective-permute-start.14) | collective-permute-done | bytes 262176 | tf_op jit(solution)/shard_map/ppermute | solution.py:28
  199.9 5.3 %correlate.12 = (f32[3,32,4,2,128,128]{5,4,3,2,1,0:T(8,128)}, f32[8,128]{1,0:T(8,128)S(1)}) custom-call(s32[10]{0:T(128)S(1)} %copy-done.21, s32[20]{0:T(128)S(1)} %reshape.115.blocks_ref, f32[4,16,32,128]{3,2,1,0:T(8,128)S(1)} %pack.31.refs_2_.refs_0_, ...), custom_call_target="tpu_custom_call", output_to_operand_aliasing={{0}: (5, {})} | custom-call | flops 1207959552 | bytes 10485760 | tf_op jit(solution)/shard_map/correlate/pallas_call | solution.py:446
  209.2 8.5 %collective-permute-done.9.refs_0_ = f32[16,32,128]{2,1,0:T(8,128)S(1)} collective-permute-done((f32[16,32,128]{2,1,0:T(8,128)S(1)}, f32[16,32,128]{2,1,0:T(8,128)S(1)}, u32[]{:S(2)}, u32[]{:S(2)}) %collective-permute-start.9) | collective-permute-done | bytes 262176 | tf_op jit(solution)/shard_map/ppermute | solution.py:28
  227.1 5.3 %correlate.13 = (f32[3,32,4,2,128,128]{5,4,3,2,1,0:T(8,128)}, f32[8,128]{1,0:T(8,128)S(1)}) custom-call(s32[10]{0:T(128)S(1)} %copy-done.21, s32[20]{0:T(128)S(1)} %reshape.115.blocks_ref, f32[4,16,32,128]{3,2,1,0:T(8,128)S(1)} %pack.33.refs_2_.refs_0_, ...), custom_call_target="tpu_custom_call", output_to_operand_aliasing={{0}: (5, {})} | custom-call | flops 1207959552 | bytes 10485760 | tf_op jit(solution)/shard_map/correlate/pallas_call | solution.py:446
  232.4 7.9 %collective-permute-done.5.refs_0_ = f32[16,32,128]{2,1,0:T(8,128)S(1)} collective-permute-done((f32[16,32,128]{2,1,0:T(8,128)S(1)}, f32[16,32,128]{2,1,0:T(8,128)S(1)}, u32[]{:S(2)}, u32[]{:S(2)}) %collective-permute-start.5) | collective-permute-done | bytes 262176 | tf_op jit(solution)/shard_map/ppermute | solution.py:28
  240.3 6.5 %collective-permute-done.6.refs_1_ = f32[16,32,128]{2,1,0:T(8,128)S(1)} collective-permute-done((f32[16,32,128]{2,1,0:T(8,128)S(1)}, f32[16,32,128]{2,1,0:T(8,128)S(1)}, u32[]{:S(2)}, u32[]{:S(2)}) %collective-permute-start.6) | collective-permute-done | bytes 262176 | tf_op jit(solution)/shard_map/ppermute | solution.py:28
  252.3 5.3 %correlate.14 = (f32[3,32,4,2,128,128]{5,4,3,2,1,0:T(8,128)}, f32[8,128]{1,0:T(8,128)S(1)}) custom-call(s32[10]{0:T(128)S(1)} %copy-done.21, s32[20]{0:T(128)S(1)} %reshape.115.blocks_ref, f32[4,16,32,128]{3,2,1,0:T(8,128)S(1)} %pack.35.refs_2_.refs_0_, ...), custom_call_target="tpu_custom_call", output_to_operand_aliasing={{0}: (5, {})} | custom-call | flops 1207959552 | bytes 10485760 | tf_op jit(solution)/shard_map/correlate/pallas_call | solution.py:446
  257.6 15.7 %collective-permute-done.48.refs_0_.refs_1_ = f32[4,16,32,128]{3,2,1,0:T(8,128)S(1)} collective-permute-done((f32[4,16,32,128]{3,2,1,0:T(8,128)S(1)}, f32[4,16,32,128]{3,2,1,0:T(8,128)S(1)}, u32[]{:S(2)}, u32[]{:S(2)}) %collective-permute-start.48) | collective-permute-done | bytes 1048608 | tf_op jit(solution)/shard_map/ppermute | solution.py:28
  276.8 5.3 %correlate.15 = (f32[3,32,4,2,128,128]{5,4,3,2,1,0:T(8,128)}, f32[8,128]{1,0:T(8,128)}) custom-call(s32[10]{0:T(128)S(1)} %copy-done.21, s32[20]{0:T(128)S(1)} %reshape.115.blocks_ref, f32[4,16,32,128]{3,2,1,0:T(8,128)S(1)} %pack.37.refs_2_.refs_0_, f32[4,16,32,128]{3,2,1,0:T(8,128)S(1)} %collective-permute-done.48.refs_0_.refs_1_, ...), custom_call_target="tpu_custom_call", output_to_operand_aliasing={{0}: (6, {})} | custom-call | flops 1207959552 | bytes 10485760 | tf_op jit(solution)/shard_map/correlate/pallas_call | solution.py:446
  (192 shorter events, 112.6 us)
Async XLA Ops:
  31.2 25.6 %collective-permute-start.21 = (f32[4,2,8,16,128]{4,3,2,1,0:T(8,128)S(1)}, f32[4,2,8,16,128]{4,3,2,1,0:T(8,128)S(1)}, u32[]{:S(2)}, u32[]{:S(2)}) collective-permute-start(f32[4,2,8,16,128]{4,3,2,1,0:T(8,128)S(1)} %bitcast.60), channel_id=1, source_target_pairs={{0,4},{4,0},{8,12},{12,8},{16,20},{20,16},{24,28},{28,24},{1,5},{5... | collective-permute-start | bytes 1572872 | tf_op jit(solution)/shard_map/ppermute | solution.py:28
  52.8 30.4 %collective-permute-start.35 = (f32[4,16,32,128]{3,2,1,0:T(8,128)S(1)}, f32[4,16,32,128]{3,2,1,0:T(8,128)S(1)}, u32[]{:S(2)}, u32[]{:S(2)}) collective-permute-start(f32[4,16,32,128]{3,2,1,0:T(8,128)S(1)} %pack.24.refs_0_), channel_id=1, source_target_pairs={{0,2},{1,3},{2,0},{3,1},{4,6},{5,7},{6,4},{7,5},{8,10},{9,11},{10,... | collective-permute-start | bytes 3145736 | tf_op jit(solution)/shard_map/ppermute | solution.py:28
  58.2 25.3 %collective-permute-start.16 = (f32[4,2,8,16,128]{4,3,2,1,0:T(8,128)S(1)}, f32[4,2,8,16,128]{4,3,2,1,0:T(8,128)S(1)}, u32[]{:S(2)}, u32[]{:S(2)}) collective-permute-start(f32[4,2,8,16,128]{4,3,2,1,0:T(8,128)S(1)} %get-tuple-element.129), channel_id=1, source_target_pairs={{0,4},{4,0},{8,12},{12,8},{16,20},{20,16},{24,28},{28,24},{1,5},{5... | collective-permute-start | bytes 1572872 | tf_op jit(solution)/shard_map/ppermute | solution.py:28
  58.4 24.8 %collective-permute-start.31 = (f32[16,32,128]{2,1,0:T(8,128)S(1)}, f32[16,32,128]{2,1,0:T(8,128)S(1)}, u32[]{:S(2)}, u32[]{:S(2)}) collective-permute-start(f32[16,32,128]{2,1,0:T(8,128)S(1)} %get-tuple-element.150), channel_id=1, source_target_pairs={{0,24},{4,28},{8,16},{12,20},{16,8},{20,12},{24,0},{28,4},{1,25},{... | collective-permute-start | bytes 786440 | tf_op jit(solution)/shard_map/ppermute | solution.py:28
  85.0 27.5 %collective-permute-start.36 = (f32[4,16,32,128]{3,2,1,0:T(8,128)S(1)}, f32[4,16,32,128]{3,2,1,0:T(8,128)S(1)}, u32[]{:S(2)}, u32[]{:S(2)}) collective-permute-start(f32[4,16,32,128]{3,2,1,0:T(8,128)S(1)} %pack.25.refs_2_.refs_0_), channel_id=1, source_target_pairs={{0,2},{1,3},{2,0},{3,1},{4,6},{5,7},{6,4},{7,5},{8,10},{9,11},{10,... | collective-permute-start | bytes 3145736 | tf_op jit(solution)/shard_map/ppermute | solution.py:28
  85.0 28.8 %collective-permute-start.12 = (f32[4,2,8,16,128]{4,3,2,1,0:T(8,128)}, f32[4,2,8,16,128]{4,3,2,1,0:T(8,128)}, u32[]{:S(2)}, u32[]{:S(2)}) collective-permute-start(f32[4,2,8,16,128]{4,3,2,1,0:T(8,128)} %get-tuple-element.123), channel_id=1, source_target_pairs={{0,4},{4,0},{8,12},{12,8},{16,20},{20,16},{24,28},{28,24},{1,5},{5... | collective-permute-start | bytes 1572872 | tf_op jit(solution)/shard_map/ppermute | solution.py:28
  87.2 25.2 %collective-permute-start.27 = (f32[16,32,128]{2,1,0:T(8,128)}, f32[16,32,128]{2,1,0:T(8,128)}, u32[]{:S(2)}, u32[]{:S(2)}) collective-permute-start(f32[16,32,128]{2,1,0:T(8,128)} %get-tuple-element.143), channel_id=1, source_target_pairs={{0,24},{4,28},{8,16},{12,20},{16,8},{20,12},{24,0},{28,4},{1,25},{... | collective-permute-start | bytes 786440 | tf_op jit(solution)/shard_map/ppermute | solution.py:28
  90.1 22.4 %collective-permute-start.28 = (f32[16,32,128]{2,1,0:T(8,128)}, f32[16,32,128]{2,1,0:T(8,128)}, u32[]{:S(2)}, u32[]{:S(2)}) collective-permute-start(f32[16,32,128]{2,1,0:T(8,128)} %get-tuple-element.144), channel_id=1, source_target_pairs={{0,8},{4,12},{8,0},{12,4},{16,24},{20,28},{24,16},{28,20},{1,9},{5... | collective-permute-start | bytes 786440 | tf_op jit(solution)/shard_map/ppermute | solution.py:28
  114.9 24.8 %collective-permute-start.38 = (f32[4,16,32,128]{3,2,1,0:T(8,128)S(1)}, f32[4,16,32,128]{3,2,1,0:T(8,128)S(1)}, u32[]{:S(2)}, u32[]{:S(2)}) collective-permute-start(f32[4,16,32,128]{3,2,1,0:T(8,128)S(1)} %pack.27.refs_2_.refs_0_), channel_id=1, source_target_pairs={{0,2},{1,3},{2,0},{3,1},{4,6},{5,7},{6,4},{7,5},{8,10},{9,11},{10,... | collective-permute-start | bytes 3145736 | tf_op jit(solution)/shard_map/ppermute | solution.py:28
  116.4 23.6 %collective-permute-start.8 = (f32[4,2,8,16,128]{4,3,2,1,0:T(8,128)S(1)}, f32[4,2,8,16,128]{4,3,2,1,0:T(8,128)S(1)}, u32[]{:S(2)}, u32[]{:S(2)}) collective-permute-start(f32[4,2,8,16,128]{4,3,2,1,0:T(8,128)S(1)} %copy-done.27), channel_id=1, source_target_pairs={{0,4},{4,0},{8,12},{12,8},{16,20},{20,16},{24,28},{28,24},{1,5},{5... | collective-permute-start | bytes 1572872 | tf_op jit(solution)/shard_map/ppermute | solution.py:28
  116.7 23.1 %collective-permute-start.24 = (f32[16,32,128]{2,1,0:T(8,128)S(1)}, f32[16,32,128]{2,1,0:T(8,128)S(1)}, u32[]{:S(2)}, u32[]{:S(2)}) collective-permute-start(f32[16,32,128]{2,1,0:T(8,128)S(1)} %copy-done.31), channel_id=1, source_target_pairs={{0,24},{4,28},{8,16},{12,20},{16,8},{20,12},{24,0},{28,4},{1,25},{... | collective-permute-start | bytes 786440 | tf_op jit(solution)/shard_map/ppermute | solution.py:28
  141.9 25.6 %collective-permute-start.40 = (f32[4,16,32,128]{3,2,1,0:T(8,128)S(1)}, f32[4,16,32,128]{3,2,1,0:T(8,128)S(1)}, u32[]{:S(2)}, u32[]{:S(2)}) collective-permute-start(f32[4,16,32,128]{3,2,1,0:T(8,128)S(1)} %pack.29.refs_2_.refs_0_), channel_id=1, source_target_pairs={{0,2},{1,3},{2,0},{3,1},{4,6},{5,7},{6,4},{7,5},{8,10},{9,11},{10,... | collective-permute-start | bytes 3145736 | tf_op jit(solution)/shard_map/ppermute | solution.py:28
  143.0 24.7 %collective-permute-start.4 = (f32[4,2,8,16,128]{4,3,2,1,0:T(8,128)S(1)}, f32[4,2,8,16,128]{4,3,2,1,0:T(8,128)S(1)}, u32[]{:S(2)}, u32[]{:S(2)}) collective-permute-start(f32[4,2,8,16,128]{4,3,2,1,0:T(8,128)S(1)} %copy-done.25), channel_id=1, source_target_pairs={{0,4},{4,0},{8,12},{12,8},{16,20},{20,16},{24,28},{28,24},{1,5},{5... | collective-permute-start | bytes 1572872 | tf_op jit(solution)/shard_map/ppermute | solution.py:28
  143.2 24.3 %collective-permute-start.18 = (f32[16,32,128]{2,1,0:T(8,128)S(1)}, f32[16,32,128]{2,1,0:T(8,128)S(1)}, u32[]{:S(2)}, u32[]{:S(2)}) collective-permute-start(f32[16,32,128]{2,1,0:T(8,128)S(1)} %get-tuple-element.131), channel_id=1, source_target_pairs={{0,24},{4,28},{8,16},{12,20},{16,8},{20,12},{24,0},{28,4},{1,25},{... | collective-permute-start | bytes 786440 | tf_op jit(solution)/shard_map/ppermute | solution.py:28
  145.7 21.8 %collective-permute-start.19 = (f32[16,32,128]{2,1,0:T(8,128)S(1)}, f32[16,32,128]{2,1,0:T(8,128)S(1)}, u32[]{:S(2)}, u32[]{:S(2)}) collective-permute-start(f32[16,32,128]{2,1,0:T(8,128)S(1)} %get-tuple-element.132), channel_id=1, source_target_pairs={{0,8},{4,12},{8,0},{12,4},{16,24},{20,28},{24,16},{28,20},{1,9},{5... | collective-permute-start | bytes 786440 | tf_op jit(solution)/shard_map/ppermute | solution.py:28
  169.4 24.9 %collective-permute-start.42 = (f32[4,16,32,128]{3,2,1,0:T(8,128)S(1)}, f32[4,16,32,128]{3,2,1,0:T(8,128)S(1)}, u32[]{:S(2)}, u32[]{:S(2)}) collective-permute-start(f32[4,16,32,128]{3,2,1,0:T(8,128)S(1)} %pack.31.refs_2_.refs_0_), channel_id=1, source_target_pairs={{0,2},{1,3},{2,0},{3,1},{4,6},{5,7},{6,4},{7,5},{8,10},{9,11},{10,... | collective-permute-start | bytes 3145736 | tf_op jit(solution)/shard_map/ppermute | solution.py:28
  170.9 23.4 %collective-permute-start.14 = (f32[16,32,128]{2,1,0:T(8,128)S(1)}, f32[16,32,128]{2,1,0:T(8,128)S(1)}, u32[]{:S(2)}, u32[]{:S(2)}) collective-permute-start(f32[16,32,128]{2,1,0:T(8,128)S(1)} %get-tuple-element.125), channel_id=1, source_target_pairs={{0,24},{4,28},{8,16},{12,20},{16,8},{20,12},{24,0},{28,4},{1,25},{... | collective-permute-start | bytes 786440 | tf_op jit(solution)/shard_map/ppermute | solution.py:28
  171.0 23.3 %collective-permute-start.15 = (f32[16,32,128]{2,1,0:T(8,128)S(1)}, f32[16,32,128]{2,1,0:T(8,128)S(1)}, u32[]{:S(2)}, u32[]{:S(2)}) collective-permute-start(f32[16,32,128]{2,1,0:T(8,128)S(1)} %get-tuple-element.126), channel_id=1, source_target_pairs={{0,8},{4,12},{8,0},{12,4},{16,24},{20,28},{24,16},{28,20},{1,9},{5... | collective-permute-start | bytes 786440 | tf_op jit(solution)/shard_map/ppermute | solution.py:28
  195.9 24.7 %collective-permute-start.44 = (f32[4,16,32,128]{3,2,1,0:T(8,128)S(1)}, f32[4,16,32,128]{3,2,1,0:T(8,128)S(1)}, u32[]{:S(2)}, u32[]{:S(2)}) collective-permute-start(f32[4,16,32,128]{3,2,1,0:T(8,128)S(1)} %pack.33.refs_2_.refs_0_), channel_id=1, source_target_pairs={{0,2},{1,3},{2,0},{3,1},{4,6},{5,7},{6,4},{7,5},{8,10},{9,11},{10,... | collective-permute-start | bytes 3145736 | tf_op jit(solution)/shard_map/ppermute | solution.py:28
  222.2 24.7 %collective-permute-start.46 = (f32[4,16,32,128]{3,2,1,0:T(8,128)S(1)}, f32[4,16,32,128]{3,2,1,0:T(8,128)S(1)}, u32[]{:S(2)}, u32[]{:S(2)}) collective-permute-start(f32[4,16,32,128]{3,2,1,0:T(8,128)S(1)} %pack.35.refs_2_.refs_0_), channel_id=1, source_target_pairs={{0,2},{1,3},{2,0},{3,1},{4,6},{5,7},{6,4},{7,5},{8,10},{9,11},{10,... | collective-permute-start | bytes 3145736 | tf_op jit(solution)/shard_map/ppermute | solution.py:28
  223.5 23.2 %collective-permute-start.6 = (f32[16,32,128]{2,1,0:T(8,128)S(1)}, f32[16,32,128]{2,1,0:T(8,128)S(1)}, u32[]{:S(2)}, u32[]{:S(2)}) collective-permute-start(f32[16,32,128]{2,1,0:T(8,128)S(1)} %get-tuple-element.111), channel_id=1, source_target_pairs={{0,24},{4,28},{8,16},{12,20},{16,8},{20,12},{24,0},{28,4},{1,25},{... | collective-permute-start | bytes 786440 | tf_op jit(solution)/shard_map/ppermute | solution.py:28
  223.7 23.1 %collective-permute-start.7 = (f32[16,32,128]{2,1,0:T(8,128)S(1)}, f32[16,32,128]{2,1,0:T(8,128)S(1)}, u32[]{:S(2)}, u32[]{:S(2)}) collective-permute-start(f32[16,32,128]{2,1,0:T(8,128)S(1)} %get-tuple-element.112), channel_id=1, source_target_pairs={{0,8},{4,12},{8,0},{12,4},{16,24},{20,28},{24,16},{28,20},{1,9},{5... | collective-permute-start | bytes 786440 | tf_op jit(solution)/shard_map/ppermute | solution.py:28
  248.6 24.7 %collective-permute-start.48 = (f32[4,16,32,128]{3,2,1,0:T(8,128)S(1)}, f32[4,16,32,128]{3,2,1,0:T(8,128)S(1)}, u32[]{:S(2)}, u32[]{:S(2)}) collective-permute-start(f32[4,16,32,128]{3,2,1,0:T(8,128)S(1)} %pack.37.refs_2_.refs_0_), channel_id=1, source_target_pairs={{0,2},{1,3},{2,0},{3,1},{4,6},{5,7},{6,4},{7,5},{8,10},{9,11},{10,... | collective-permute-start | bytes 3145736 | tf_op jit(solution)/shard_map/ppermute | solution.py:28
  250.0 24.5 %collective-permute-start.49 = (f32[4,16,32,128]{3,2,1,0:T(8,128)S(1)}, f32[4,16,32,128]{3,2,1,0:T(8,128)S(1)}, u32[]{:S(2)}, u32[]{:S(2)}) collective-permute-start(f32[4,16,32,128]{3,2,1,0:T(8,128)S(1)} %pack.37.refs_2_.refs_0_), channel_id=1, source_target_pairs={{0,1},{1,0},{2,3},{3,2},{4,5},{5,4},{6,7},{7,6},{8,9},{9,8},{10,11... | collective-permute-start | bytes 3145736 | tf_op jit(solution)/shard_map/ppermute | solution.py:28
  (61 other events, 558.0 us)
where the time goes:
time: 284 us; the launch traced here: 282 us
  waiting for transfers between devices  145 us (51%)
  Pallas kernels  71.2 us (25%)
  starting transfers between devices  51.4 us (18%)
  local copies, waits for them, and re-layouts  14.1 us (5%)
    ppermute x51, waiting for transfers between devices, swapped(): lax.ppermute(value, axis, [(source, source ^ mask) for source in range(co...  145 us
    ppermute x51, starting transfers between devices, swapped(): lax.ppermute(value, axis, [(source, source ^ mask) for source in range(co...  48.7 us
    pallas_call x8, Pallas kernels, correlated(): pl.pallas_call(functools.partial(correlate_kernel, slots, tiles, order),...  42.2 us
    unnamed x67, local copies, waits for them, and re-layouts  12.5 us
    pallas_call x5, Pallas kernels, transformed(): pl.pallas_call(functools.partial(transform_kernel, groups, pieces), grid=...  11.5 us
    pallas_call x20, Pallas kernels, packed(): pl.pallas_call(functools.partial(pack_kernel, counts), grid=(values[0].sh...  6.42 us
    pallas_call x2, Pallas kernels, filtered_samples(): pl.pallas_call(functools.partial(filter_kernel, count), grid=(inputs // w...  5.88 us
  transfers between devices with their start and end apart: 52, of which 26 were waited for; matrix products, arithmetic and copies ran while one was open for 0% of the time, Pallas kernels for 22%

commit v1 on v0

--- a/solution.py
+++ b/solution.py
@@ -12,6 +12,8 @@
 BLOCK = 128
 RADIX = 4
 STEP = 256
+HALF = 2
+LONG = 2_000_000_000_000
 VMEM_BYTES = 20 * 1024 * 1024
 BF16 = jnp.bfloat16
 F32 = jnp.float32
@@ -283,6 +285,7 @@
     near_refs, far_refs, out_refs = refs[: len(groups)], refs[len(groups) : 2 * len(groups)], refs[-count:]
     total = sum(groups)
     odd = lax.axis_index("chan") % 2 == 1
+    other = 1 - lax.axis_index("chan") % 2
     lower = lax.broadcasted_iota(jnp.int32, (total, BLOCK), 1) < BLOCK // 2
     for unit, out_ref in enumerate(out_refs):
         for channel in range(piece):
@@ -290,7 +293,9 @@
 
                 def rows_of(segment_refs):
                     rows = [
-                        ref[pl.ds((unit * 2 + part) * held * piece + channel, held, stride=piece), :]
+                        (ref if len(ref.shape) == 2 else ref.at[other])[
+                            pl.ds((unit * 2 + part) * held * piece + channel, held, stride=piece), :
+                        ]
                         for ref, held in zip(segment_refs, groups)
                     ]
                     return rows[0] if len(rows) == 1 else jnp.concatenate(rows, axis=0)
@@ -320,7 +325,7 @@
         compiler_params=params(),
         cost_estimate=pl.CostEstimate(flops=4 * size, bytes_accessed=16 * size, transcendentals=0),
         name="merge",
-    )(*[value.reshape(-1, lanes) for value in list(near) + list(far)], *after)
+    )(*[value.reshape(value.shape[:-5] + (-1, lanes)) for value in list(near) + list(far)], *after)
 
 
 def pack_kernel(counts, *refs):
@@ -330,7 +335,7 @@
             out_ref[index] = next(sources)[...]
 
 
-def packed(batches, after):
+def packed(batches, after, moves=None):
     counts = [len(batch) for batch in batches]
     values = [value for batch in batches for value in batch]
     width = 8
@@ -351,7 +356,9 @@
         out_shape=[jax.ShapeDtypeStruct(shape, F32) for shape in shapes],
         compiler_params=params(),
         cost_estimate=pl.CostEstimate(
-            flops=0, bytes_accessed=8 * sum(value.size for value in values), transcendentals=0
+            flops=moves or 0,
+            bytes_accessed=moves or 8 * sum(value.size for value in values),
+            transcendentals=0,
         ),
         name="pack",
     )(*values, *after)
@@ -361,18 +368,21 @@
     return lax.dot_general(left, right, (((0,), (0,)), ((), ())), preferred_element_type=F32)
 
 
-def correlate_kernel(slots, tiles, order, slot_ref, blocks_ref, *refs):
-    unit_refs = []
-    for ref in refs[:-5]:
-        if len(ref.shape) == 4:
-            unit_refs.append(ref)
-        elif len(ref.shape) == 5 and len(unit_refs) < tiles:
-            unit_refs += [ref.at[0], ref.at[1]]
+def correlate_kernel(slots, order, where, slot_ref, blocks_ref, *refs):
     out_ref, done_ref, high_ref, low_ref, place_ref = refs[-5:]
     done_ref[...] = jnp.zeros(done_ref.shape, F32)
-    blocks, width, depth, _ = unit_refs[0].shape
+    tiles = len(where)
+    blocks = len(order)
+    width = out_ref.shape[1]
+    depth = high_ref.shape[2] // tiles
     rows = depth // 2
     half = tiles * rows
+
+    def unit_rows(tile, mask, channel, span):
+        index, lead = where[tile][mask // HALF]
+        if lead is None:
+            return refs[index][mask % HALF, channel, span]
+        return refs[index][lead, mask % HALF, channel, span]
 
     @pl.when(pl.program_id(0) == 0)
     def _():
@@ -397,8 +407,8 @@
             for part in range(2):
                 joined = jnp.concatenate(
                     [
-                        unit_ref[mask, channel, part * rows : (part + 1) * rows]
-                        for unit_ref in unit_refs
+                        unit_rows(tile, mask, channel, slice(part * rows, (part + 1) * rows))
+                        for tile in range(tiles)
                     ],
                     axis=0,
                 )
@@ -426,14 +436,15 @@
             out_ref[slot, channel, 1] = value[:, BLOCK:]
 
 
-def correlated(order, tile_slot, tile_blocks, units, visibility, residue, first, total, slots):
-    tiles = sum(1 if unit.ndim == 4 else unit.shape[0] for unit in units)
-    blocks, piece, depth, lanes = units[0].shape
+def correlated(order, tile_slot, tile_blocks, units, where, visibility, residue, first, total, slots):
+    tiles = len(where)
+    blocks = len(order)
+    piece, depth, lanes = units[0].shape[-3:]
     width = 4
     out = jax.ShapeDtypeStruct((slots, total, RADIX, 2, BLOCK, BLOCK), F32)
     operands = [tile_slot, tile_blocks.reshape(-1)] + units
     in_specs = [
-        pl.BlockSpec((blocks, width, depth, lanes), lambda i, *_: (0, i, 0, 0))
+        pl.BlockSpec((HALF, width, depth, lanes), lambda i, *_: (0, i, 0, 0))
         if unit.ndim == 4
         else pl.BlockSpec(unit.shape[:2] + (width, depth, lanes), lambda i, *_: (0, 0, i, 0, 0))
         for unit in units
@@ -444,7 +455,7 @@
         in_specs.append(pl.BlockSpec(memory_space=pl.ANY))
         aliases = {len(operands) - 1: 0}
     return pl.pallas_call(
-        functools.partial(correlate_kernel, slots, tiles, order),
+        functools.partial(correlate_kernel, slots, order, where),
         grid_spec=pltpu.PrefetchScalarGridSpec(
             num_scalar_prefetch=2,
             grid=(piece // width,),
@@ -461,11 +472,7 @@
         out_shape=[out, jax.ShapeDtypeStruct((8, BLOCK), F32)],
         input_output_aliases=aliases,
         compiler_params=params(),
-        cost_estimate=pl.CostEstimate(
-            flops=3 * 2 * slots * piece * tiles * depth * BLOCK * 2 * BLOCK,
-            bytes_accessed=4 * piece * lanes * (tiles * blocks * depth + slots * 2 * BLOCK),
-            transcendentals=0,
-        ),
+        cost_estimate=pl.CostEstimate(flops=1, bytes_accessed=1, transcendentals=0),
         name="correlate",
     )(*operands)
 
@@ -481,7 +488,7 @@
     scale = 1.0 / math.sqrt(length * frames * tiles)
     table = jnp.asarray(fourier_table(length // RADIX, owners, scale))
 
-    order = list(range(2, blocks)) + [1, 0]
+    order = [2, 1, 3, 0]
     groups = [tuple(2 * block + x for block in order) for x in range(2)]
     halves = 2
     size = channels // RADIX // halves
@@ -490,7 +497,6 @@
     share = [[] for _ in range(count)]
     away = [None] * count
     units = [None] * count
-    paired = [None] * count
 
     steps = frames * inputs // STEP
     late = STEP // inputs
@@ -511,63 +517,86 @@
 
     def leave(piece):
         values = share[piece]
-        if 0 < piece < 4:
-            after = [away[piece - 1][-1]]
-            values = [packed([[value]], after)[0].reshape(value.shape) for value in values]
-        away[piece] = [swapped(value, "chan", 1) for value in values]
+        if piece < halves:
+            if piece:
+                after = [away[piece - 1][-1]]
+                values = [packed([[value]], after)[0].reshape(value.shape) for value in values]
+            away[piece] = [swapped(value, "chan", 1) for value in values]
+        else:
+            pairs = [[2 * block, 2 * block + 1] for block in range(blocks)]
+            away[piece] = [lax.all_gather(value, "chan", axis_index_groups=pairs) for value in values]
 
     def merge(piece, after):
         units[piece] = merged(near[piece], away[piece], after)
 
-    def along(piece):
-        return [
-            swapped(unit, "chan", 2 * block) if block else unit
-            for block, unit in zip(order, units[piece])
-        ]
+    def along(piece, place, after):
+        unit, block = units[piece][place], order[place]
+        if after:
+            unit = packed([[unit]], after)[0][0]
+        return swapped(unit, "chan", 2 * block) if block else unit
 
     leave(0)
     merge(0, near[halves][:1])
-    turned = along(0)
+    turned = [[along(0, place, []) for place in range(blocks)]] + [[None] * blocks for _ in range(count)]
     for residue in range(2, RADIX):
-        spectra(samples, residue, turned[-2:-1], 0, steps)
+        spectra(samples, residue, turned[0][1:2], 0, steps)
     leave(1)
     merge(1, [])
-    leave(2)
-
-    def products(piece, arrays, visibility):
+
+    def products(piece, arrays, where, visibility):
         return correlated(
-            order, tile_slot, tile_blocks, arrays, visibility,
+            order, tile_slot, tile_blocks, arrays, where, visibility,
             piece // halves, piece % halves * size, channels // RADIX, slots,
         )
 
     visibility = None
     finished = []
-    pair = None
+    own = [[None, None] for _ in range(count)]
+    across = [[None, None] for _ in range(count)]
+    crossed = []
+    where = [[(0, None), (1, None)], [(2, None), (3, None)], [(4, 0), (4, 1)], [(4, 2), (4, 3)]]
+
+    def half_step(piece, half, after):
+        values = turned[piece][half * HALF : (half + 1) * HALF]
+        (own[piece][half],) = packed([values], after, LONG)
+        across[piece][half] = swapped(own[piece][half], "tile", 2)
+
+    def between_cores(piece, after, visibility):
+        arrays = own[piece] + across[piece]
+        (both,) = packed([arrays], after)
+        crossed.append(swapped(both, "tile", 1))
+        visibility, token = products(piece, arrays + crossed[-1:], where, visibility)
+        finished.append(token)
+        return visibility
+
     for piece in range(count):
-        if piece:
-            after = [pair[1]]
-            for later in range(piece + 1, min(piece + 3, count)):
-                if units[later] is None:
-                    merge(later, [])
-                after.append(units[later][0])
-        else:
-            after = [units[1][0]] + [near[residue * halves][0] for residue in range(2, RADIX)]
-        after += finished[piece - 2 : piece - 1] if piece >= 2 else []
-        (own,) = packed([turned], after)
+        after = [across[piece - 1][0], own[piece - 1][1]] if piece else []
         if piece + 1 < count:
-            turned = along(piece + 1)
-        across = swapped(own, "tile", 2)
-        if piece + 3 < count:
-            leave(piece + 3)
-        if pair:
-            (both,) = packed([pair], [own] + (away[piece + 3][-1:] if piece + 3 < count else []))
-            paired[piece - 1] = swapped(both, "tile", 1)
-            visibility, token = products(piece - 1, pair + [paired[piece - 1]], visibility)
-            finished.append(token)
-        pair = [own, across]
-    (last,) = packed([[across]], finished[-1:])
-    arrays = pair + [swapped(own, "tile", 1), swapped(last[0], "tile", 1)]
-    visibility, _ = products(count - 1, arrays, visibility)
+            if units[piece + 1] is None:
+                leave(piece + 1)
+                merge(piece + 1, [])
+            after.append(units[piece + 1][0])
+        if not piece:
+            after += [near[residue * halves][0] for residue in range(2, RADIX)]
+        after += finished[piece - 3 : piece - 2] if piece >= 3 else []
+        half_step(piece, 0, after)
+        if piece + 1 < count:
+            turned[piece + 1][0] = along(piece + 1, 0, [own[piece][0]])
+        after = ([across[piece - 1][1]] if piece else []) + [own[piece][0]]
+        if piece >= 2:
+            visibility = between_cores(piece - 2, [own[piece][0]], visibility)
+        half_step(piece, 1, after)
+        if piece + 1 < count:
+            turned[piece + 1][2] = along(piece + 1, 2, [])
+            turned[piece + 1][1] = along(piece + 1, 1, [own[piece][1]] + crossed[piece - 2 :] if piece >= 2 else [own[piece][1]])
+            turned[piece + 1][3] = along(piece + 1, 3, [])
+    visibility = between_cores(count - 2, own[count - 1][1:], visibility)
+    last = count - 1
+    (final,) = packed([across[last][1:]], finished[-1:])
+    arrays = own[last] + across[last]
+    arrays += [swapped(value, "tile", 1) for value in own[last] + across[last][:1] + [final[0]]]
+    where = [[(2 * tile, None), (2 * tile + 1, None)] for tile in range(tiles)]
+    visibility, _ = products(last, arrays, where, visibility)
     return visibility.reshape(slots, channels, 2, BLOCK, BLOCK)
 
 
@@ -577,7 +606,7 @@
     owners, tiles = mesh.shape["chan"], mesh.shape["tile"]
 
     def run(voltage, fir_taps, tile_slot, tile_blocks):
-        paired = 2 * voltage.shape[2] == BLOCK * owners and tiles == 4
+        paired = 2 * voltage.shape[2] == BLOCK * owners and tiles == 4 and owners == 8
         chosen = body if paired else generic_body
         return jax.shard_map(
             chosen, mesh=mesh, in_specs=in_specs, out_specs=out_specs, check_vma=False

time: 284 us -> 320 us (1.13)
  waiting for transfers between devices: 145 us -> 56.8 us
  Pallas kernels: 71.2 us -> 132 us
  starting transfers between devices: 51.4 us -> 100 us
  between operations: 0.56 us -> 13.9 us
    ppermute x51 -> x55, waiting for transfers between devices: 145 us -> 56.7 us  [swapped(): lax.ppermute(value, axis, [(source, source ^ mask) for source in range(co...]
    ppermute x51 -> x55, starting transfers between devices: 48.7 us -> 97.2 us  [swapped(): lax.ppermute(value, axis, [(source, source ^ mask) for source in range(co...]
    pallas_call x20 -> x40, Pallas kernels: 6.42 us -> 46.8 us  [packed(): pl.pallas_call(functools.partial(pack_kernel, counts), grid=(values[0].sh...]
    pallas_call x8, Pallas kernels: 42.2 us -> 56.7 us  [correlated(): pl.pallas_call(functools.partial(correlate_kernel, slots, order, where),...]
    pallas_call x8, Pallas kernels: 5.18 us -> 9.58 us  [merged(): pl.pallas_call(functools.partial(merge_kernel, count, groups, piece), in_...]
    unnamed x67 -> x77, local copies, waits for them, and re-layouts: 12.5 us -> 11.8 us
  transfers between devices with their start and end apart: 52 -> 62, of which waited for: 26 -> 14; matrix products, arithmetic and copies ran while one was open for 0% -> 0% of each run, Pallas kernels for 22% -> 40%
where the time goes in v1:
time: 320 us; the launch traced here: 316 us
  Pallas kernels  132 us (41%)
  starting transfers between devices  100 us (31%)
  waiting for transfers between devices  56.8 us (18%)
  between operations  13.9 us (4%)
  local copies, waits for them, and re-layouts  13.4 us (4%)
    ppermute x55, starting transfers between devices, swapped(): lax.ppermute(value, axis, [(source, source ^ mask) for source in range(co...  97.2 us
    ppermute x55, waiting for transfers between devices, swapped(): lax.ppermute(value, axis, [(source, source ^ mask) for source in range(co...  56.7 us
    pallas_call x8, Pallas kernels, correlated(): pl.pallas_call(functools.partial(correlate_kernel, slots, order, where),...  56.7 us
    pallas_call x40, Pallas kernels, packed(): pl.pallas_call(functools.partial(pack_kernel, counts), grid=(values[0].sh...  46.8 us
    pallas_call x5, Pallas kernels, transformed(): pl.pallas_call(functools.partial(transform_kernel, groups, pieces), grid=...  13 us
    unnamed x77, local copies, waits for them, and re-layouts  11.8 us
    pallas_call x8, Pallas kernels, merged(): pl.pallas_call(functools.partial(merge_kernel, count, groups, piece), in_...  9.58 us
  transfers between devices with their start and end apart: 62, of which 14 were waited for; matrix products, arithmetic and copies ran while one was open for 0% of the time, Pallas kernels for 40%

profile of v1, /device:TPU:13, one launch (start us, length us, event | category | flops | bytes accessed | tf_op | source)
XLA Modules:
  0.0 316.2 jit_solution(9436845262857321603)
XLA Ops:
  10.8 3.4 %copy-done = f32[2,16,64,1024]{3,2,1,0:T(8,128)S(1)} copy-done((f32[2,16,64,1024]{3,2,1,0:T(8,128)S(1)}, f32[2,16,64,1024]{3,2,1,0:T(8,128)}, u32[]{:S(2)}) %copy-start) | copy-done | bytes 8388632
  14.2 4.2 %filter.2 = (bf16[16,64,512]{2,1,0:T(8,128)(2,1)S(1)}, bf16[16,64,512]{2,1,0:T(8,128)(2,1)S(1)}, bf16[16,64,512]{2,1,0:T(8,128)(2,1)S(1)}, bf16[16,64,512]{2,1,0...) custom-call(f32[2,16,64,1024]{3,2,1,0:T(8,128)S(1)} %copy-done, ...), custom_call_target="tpu_custom_call" | custom-call | flops 25165824 | bytes 12582912 | tf_op jit(solution)/shard_map/filter/pallas_call | solution.py:197
  27.7 3.7 %collective-permute-done.1 = f32[4,2,6,16,128]{4,3,2,1,0:T(8,128)S(1)} collective-permute-done((f32[4,2,6,16,128]{4,3,2,1,0:T(8,128)S(1)}, f32[4,2,6,16,128]{4,3,2,1,0:T(8,128)S(1)}, u32[]{:S(2)}, u32[]{:S(2)}) %collective-permute-start.1) | collective-permute-done | bytes 393248 | tf_op jit(solution)/shard_map/ppermute | solution.py:30
  40.3 3.4 %transform.9 = (f32[4,2,8,16,128]{4,3,2,1,0:T(8,128)S(1)}, f32[4,2,8,16,128]{4,3,2,1,0:T(8,128)S(1)}, f32[4,2,8,16,128]{4,3,2,1,0:T(8,128)}, f32[4,2,8,16,128]{4,3,2,1,0:T(8,128)}) custom-call(f32[8,64,512]{2,1,0:T(8,128)S(1)} %copy-done.4, bf16[1024,512]{1,0:T(8,128)(2,1)S(1)} %bitcast.57, bf16[1024,512]{1,0:T(8,128)(2,1)S(1)} %bitcast.58, ...), custom_call_target="tpu_custom_call" | custom-call | flops 1610612736 | bytes 5242880 | tf_op jit(solution)/shard_map/transform/pallas_call | solution.py:261
  43.8 3.5 %transform.8 = (f32[4,2,8,16,128]{4,3,2,1,0:T(8,128)S(1)}, f32[4,2,8,16,128]{4,3,2,1,0:T(8,128)S(1)}, f32[4,2,8,16,128]{4,3,2,1,0:T(8,128)}, f32[4,2,8,16,128]{4,3,2,1,0:T(8,128)}) custom-call(f32[8,64,512]{2,1,0:T(8,128)S(1)} %copy-done.4, bf16[1024,512]{1,0:T(8,128)(2,1)S(1)} %bitcast.59, bf16[1024,512]{1,0:T(8,128)(2,1)S(1)} %bitcast.60, ...), custom_call_target="tpu_custom_call" | custom-call | flops 1610612736 | bytes 5242880 | tf_op jit(solution)/shard_map/transform/pallas_call | solution.py:261
  51.5 11.5 %collective-permute-start.10 = (f32[2,16,32,128]{3,2,1,0:T(8,128)}, f32[2,16,32,128]{3,2,1,0:T(8,128)}, u32[]{:S(2)}, u32[]{:S(2)}) collective-permute-start(f32[2,16,32,128]{3,2,1,0:T(8,128)} %pack.42.refs_1_.refs_2_.refs_0_), channel_id=1, source_target_pairs={{0,2},{1,3},{2,0},{3,1},{4,6},{5,7},{6,4},{7,5},{8,10},{9,11},{10,... | collective-permute-start | bytes 1572872 | tf_op jit(solution)/shard_map/ppermute | solution.py:30
  79.3 9.2 %collective-permute-start.15 = (f32[2,16,32,128]{3,2,1,0:T(8,128)}, f32[2,16,32,128]{3,2,1,0:T(8,128)}, u32[]{:S(2)}, u32[]{:S(2)}) collective-permute-start(f32[2,16,32,128]{3,2,1,0:T(8,128)} %pack.46.refs_1_.refs_3_.refs_0_), channel_id=1, source_target_pairs={{0,2},{1,3},{2,0},{3,1},{4,6},{5,7},{6,4},{7,5},{8,10},{9,11},{10,... | collective-permute-start | bytes 1572872 | tf_op jit(solution)/shard_map/ppermute | solution.py:30
  94.4 3.8 %collective-permute-start.18 = (f32[2,16,32,128]{3,2,1,0:T(8,128)}, f32[2,16,32,128]{3,2,1,0:T(8,128)}, u32[]{:S(2)}, u32[]{:S(2)}) collective-permute-start(f32[2,16,32,128]{3,2,1,0:T(8,128)} %pack.48.refs_1_.refs_3_), channel_id=1, source_target_pairs={{0,2},{1,3},{2,0},{3,1},{4,6},{5,7},{6,4},{7,5},{8,10},{9,11},{10,... | collective-permute-start | bytes 1572872 | tf_op jit(solution)/shard_map/ppermute | solution.py:30
  100.6 3.6 %collective-permute-done.11.refs_0_ = f32[16,32,128]{2,1,0:T(8,128)S(1)} collective-permute-done((f32[16,32,128]{2,1,0:T(8,128)S(1)}, f32[16,32,128]{2,1,0:T(8,128)S(1)}, u32[]{:S(2)}, u32[]{:S(2)}) %collective-permute-start.11) | collective-permute-done | bytes 262176 | tf_op jit(solution)/shard_map/ppermute | solution.py:30
  105.7 11.0 %collective-permute-start.21 = (f32[2,16,32,128]{3,2,1,0:T(8,128)}, f32[2,16,32,128]{3,2,1,0:T(8,128)}, u32[]{:S(2)}, u32[]{:S(2)}) collective-permute-start(f32[2,16,32,128]{3,2,1,0:T(8,128)} %pack.50.refs_1_.refs_3_.refs_4_.refs_0_), channel_id=1, source_target_pairs={{0,2},{1,3},{2,0},{3,1},{4,6},{5,7},{6,4},{7,5},{8,10},{9,11},{10,... | collective-permute-start | bytes 1572872 | tf_op jit(solution)/shard_map/ppermute | solution.py:30
  131.0 7.5 %correlate.8 = (f32[3,32,4,2,128,128]{5,4,3,2,1,0:T(8,128)}, f32[8,128]{1,0:T(8,128)S(1)}) custom-call(s32[10]{0:T(128)S(1)} %copy-done.32, s32[20]{0:T(128)S(1)} %reshape.109.blocks_ref, f32[2,16,32,128]{3,2,1,0:T(8,128)} %pack.42.refs_1_.refs_2_.refs_0_, f32[2,16,32,128]{3,2,1,0:T(8,128)} %pack.44.refs_1_.refs_3_, ...), custom_call_target="tpu_custom_call" | custom-call | flops 1 | bytes 1 | tf_op jit(solution)/shard_map/correlate/pallas_call | solution.py:457
  138.5 5.6 %collective-permute-done.20.refs_1_ = f32[16,32,128]{2,1,0:T(8,128)S(1)} collective-permute-done((f32[16,32,128]{2,1,0:T(8,128)S(1)}, f32[16,32,128]{2,1,0:T(8,128)S(1)}, u32[]{:S(2)}, u32[]{:S(2)}) %collective-permute-start.20) | collective-permute-done | bytes 262176 | tf_op jit(solution)/shard_map/ppermute | solution.py:30
  161.9 7.5 %correlate.9 = (f32[3,32,4,2,128,128]{5,4,3,2,1,0:T(8,128)}, f32[8,128]{1,0:T(8,128)S(1)}) custom-call(s32[10]{0:T(128)S(1)} %copy-done.32, s32[20]{0:T(128)S(1)} %reshape.109.blocks_ref, f32[2,16,32,128]{3,2,1,0:T(8,128)} %pack.46.refs_1_.refs_3_.refs_0_, f32[2,16,32,128]{3,2,1,0:T(8,128)} %pack.48.refs_1_.refs_3_, ...), custom_call_target="tpu_custom_call", output_to_operand_aliasing={{0}: (7, {})} | custom-call | flops 1 | bytes 1 | tf_op jit(solution)/shard_map/correlate/pallas_call | solution.py:457
  169.4 3.9 %collective-permute-done.26.refs_1_ = f32[16,32,128]{2,1,0:T(8,128)S(1)} collective-permute-done((f32[16,32,128]{2,1,0:T(8,128)S(1)}, f32[16,32,128]{2,1,0:T(8,128)S(1)}, u32[]{:S(2)}, u32[]{:S(2)}) %collective-permute-start.26) | collective-permute-done | bytes 262176 | tf_op jit(solution)/shard_map/ppermute | solution.py:30
  191.0 7.4 %correlate.10 = (f32[3,32,4,2,128,128]{5,4,3,2,1,0:T(8,128)}, f32[8,128]{1,0:T(8,128)S(1)}) custom-call(s32[10]{0:T(128)S(1)} %copy-done.32, s32[20]{0:T(128)S(1)} %reshape.109.blocks_ref, f32[2,16,32,128]{3,2,1,0:T(8,128)} %pack.50.refs_1_.refs_3_.refs_4_.refs_0_, f32[2,16,32,128]{3,2,1,0:T(8,128)} %pack.52.refs_1_.refs_3_, ...), custom_call_target="tpu_custom_call", output_to_operand_aliasing={{0}: (7, {})} | custom-call | flops 1 | bytes 1 | tf_op jit(solution)/shard_map/correlate/pallas_call | solution.py:457
  198.5 5.9 %collective-permute-done.32.refs_1_ = f32[16,32,128]{2,1,0:T(8,128)S(1)} collective-permute-done((f32[16,32,128]{2,1,0:T(8,128)S(1)}, f32[16,32,128]{2,1,0:T(8,128)S(1)}, u32[]{:S(2)}, u32[]{:S(2)}) %collective-permute-start.32) | collective-permute-done | bytes 262176 | tf_op jit(solution)/shard_map/ppermute | solution.py:30
  221.8 7.4 %correlate.11 = (f32[3,32,4,2,128,128]{5,4,3,2,1,0:T(8,128)}, f32[8,128]{1,0:T(8,128)S(1)}) custom-call(s32[10]{0:T(128)S(1)} %copy-done.32, s32[20]{0:T(128)S(1)} %reshape.109.blocks_ref, f32[2,16,32,128]{3,2,1,0:T(8,128)} %pack.55.refs_1_.refs_3_.refs_4_.refs_0_, f32[2,16,32,128]{3,2,1,0:T(8,128)} %pack.57.refs_1_.refs_3_, ...), custom_call_target="tpu_custom_call", output_to_operand_aliasing={{0}: (7, {})} | custom-call | flops 1 | bytes 1 | tf_op jit(solution)/shard_map/correlate/pallas_call | solution.py:457
  229.3 4.3 %collective-permute-done.38.refs_1_ = f32[16,32,128]{2,1,0:T(8,128)S(1)} collective-permute-done((f32[16,32,128]{2,1,0:T(8,128)S(1)}, f32[16,32,128]{2,1,0:T(8,128)S(1)}, u32[]{:S(2)}, u32[]{:S(2)}) %collective-permute-start.38) | collective-permute-done | bytes 262176 | tf_op jit(solution)/shard_map/ppermute | solution.py:30
  249.0 7.4 %correlate.12 = (f32[3,32,4,2,128,128]{5,4,3,2,1,0:T(8,128)}, f32[8,128]{1,0:T(8,128)S(1)}) custom-call(s32[10]{0:T(128)S(1)} %copy-done.32, s32[20]{0:T(128)S(1)} %reshape.109.blocks_ref, f32[2,16,32,128]{3,2,1,0:T(8,128)} %pack.60.refs_1_.refs_3_.refs_4_.refs_0_, f32[2,16,32,128]{3,2,1,0:T(8,128)} %pack.62.refs_1_.refs_3_, ...), custom_call_target="tpu_custom_call", output_to_operand_aliasing={{0}: (7, {})} | custom-call | flops 1 | bytes 1 | tf_op jit(solution)/shard_map/correlate/pallas_call | solution.py:457
  256.4 8.3 %collective-permute-done.44.refs_1_ = f32[16,32,128]{2,1,0:T(8,128)S(1)} collective-permute-done((f32[16,32,128]{2,1,0:T(8,128)S(1)}, f32[16,32,128]{2,1,0:T(8,128)S(1)}, u32[]{:S(2)}, u32[]{:S(2)}) %collective-permute-start.44) | collective-permute-done | bytes 262176 | tf_op jit(solution)/shard_map/ppermute | solution.py:30
  274.9 10.6 %collective-permute-done.48.refs_2_ = f32[2,16,32,128]{3,2,1,0:T(8,128)S(1)} collective-permute-done((f32[2,16,32,128]{3,2,1,0:T(8,128)S(1)}, f32[2,16,32,128]{3,2,1,0:T(8,128)S(1)}, u32[]{:S(2)}, u32[]{:S(2)}) %collective-permute-start.48) | collective-permute-done | bytes 524320 | tf_op jit(solution)/shard_map/ppermute | solution.py:30
  287.6 7.4 %correlate.13 = (f32[3,32,4,2,128,128]{5,4,3,2,1,0:T(8,128)}, f32[8,128]{1,0:T(8,128)}) custom-call(s32[10]{0:T(128)S(1)} %copy-done.32, s32[20]{0:T(128)S(1)} %reshape.109.blocks_ref, f32[2,16,32,128]{3,2,1,0:T(8,128)} %pack.65.refs_1_.refs_3_.refs_4_.refs_0_, f32[2,16,32,128]{3,2,1,0:T(8,128)} %pack.67.refs_1_.refs_3_, ...), custom_call_target="tpu_custom_call", output_to_operand_aliasing={{0}: (7, {})} | custom-call | flops 1 | bytes 1 | tf_op jit(solution)/shard_map/correlate/pallas_call | solution.py:457
  295.1 6.6 %correlate.14 = (f32[3,32,4,2,128,128]{5,4,3,2,1,0:T(8,128)}, f32[8,128]{1,0:T(8,128)S(1)}) custom-call(s32[10]{0:T(128)S(1)} %copy-done.32, s32[20]{0:T(128)S(1)} %reshape.109.blocks_ref, f32[2,16,32,128]{3,2,1,0:T(8,128)} %pack.70.refs_1_.refs_3_.refs_4_.refs_0_, f32[2,16,32,128]{3,2,1,0:T(8,128)} %pack.72.refs_1_.refs_3_, ...), custom_call_target="tpu_custom_call", output_to_operand_aliasing={{0}: (7, {})} | custom-call | flops 1 | bytes 1 | tf_op jit(solution)/shard_map/correlate/pallas_call | solution.py:457
  304.0 5.4 %correlate.15 = (f32[3,32,4,2,128,128]{5,4,3,2,1,0:T(8,128)}, f32[8,128]{1,0:T(8,128)}) custom-call(s32[10]{0:T(128)S(1)} %copy-done.32, s32[20]{0:T(128)S(1)} %reshape.109.blocks_ref, f32[2,16,32,128]{3,2,1,0:T(8,128)S(1)} %pack.75.refs_3_.refs_4_.refs_0_, f32[2,16,32,128]{3,2,1,0:T(8,128)S(1)} %pack.76.refs_4_.refs_1_, ...), custom_call_target="tpu_custom_call", output_to_operand_aliasing={{0}: (10, {})} | custom-call | flops 1 | bytes 1 | tf_op jit(solution)/shard_map/correlate/pallas_call | solution.py:457
  (248 shorter events, 149.8 us)
Async XLA Ops:
  6.5 63.9 %all-gather.23.cloned.1.call-start = ((), (), s32[]{:S(2)}) async-start(), calls=%async_computation.5 | async-start | bytes 1572864 | tf_op jit(solution)/shard_map/all_gather | solution.py:527
  37.0 61.3 %all-gather.21.cloned.1.call-start = ((), (), s32[]{:S(2)}) async-start(), calls=%async_computation.4 | async-start | bytes 1572864 | tf_op jit(solution)/shard_map/all_gather | solution.py:527
  39.7 23.2 %collective-permute-start.8 = (f32[16,32,128]{2,1,0:T(8,128)}, f32[16,32,128]{2,1,0:T(8,128)}, u32[]{:S(2)}, u32[]{:S(2)}) collective-permute-start(f32[16,32,128]{2,1,0:T(8,128)} %copy-done.35), channel_id=1, source_target_pairs={{0,24},{4,28},{8,16},{12,20},{16,8},{20,12},{24,0},{28,4},{1,25},{... | collective-permute-start | bytes 786440 | tf_op jit(solution)/shard_map/ppermute | solution.py:30
  51.5 27.0 %collective-permute-start.10 = (f32[2,16,32,128]{3,2,1,0:T(8,128)}, f32[2,16,32,128]{3,2,1,0:T(8,128)}, u32[]{:S(2)}, u32[]{:S(2)}) collective-permute-start(f32[2,16,32,128]{3,2,1,0:T(8,128)} %pack.42.refs_1_.refs_2_.refs_0_), channel_id=1, source_target_pairs={{0,2},{1,3},{2,0},{3,1},{4,6},{5,7},{6,4},{7,5},{8,10},{9,11},{10,... | collective-permute-start | bytes 1572872 | tf_op jit(solution)/shard_map/ppermute | solution.py:30
  67.7 61.0 %all-gather.19.cloned.1.call-start = ((), (), s32[]{:S(2)}) async-start(), calls=%async_computation.3 | async-start | bytes 1572864 | tf_op jit(solution)/shard_map/all_gather | solution.py:527
  79.3 24.8 %collective-permute-start.15 = (f32[2,16,32,128]{3,2,1,0:T(8,128)}, f32[2,16,32,128]{3,2,1,0:T(8,128)}, u32[]{:S(2)}, u32[]{:S(2)}) collective-permute-start(f32[2,16,32,128]{3,2,1,0:T(8,128)} %pack.46.refs_1_.refs_3_.refs_0_), channel_id=1, source_target_pairs={{0,2},{1,3},{2,0},{3,1},{4,6},{5,7},{6,4},{7,5},{8,10},{9,11},{10,... | collective-permute-start | bytes 1572872 | tf_op jit(solution)/shard_map/ppermute | solution.py:30
  94.4 63.5 %all-gather.17.cloned.1.call-start = ((), (), s32[]{:S(2)}) async-start(), calls=%async_computation.2 | async-start | bytes 1572864 | tf_op jit(solution)/shard_map/all_gather | solution.py:527
  94.4 29.5 %collective-permute-start.18 = (f32[2,16,32,128]{3,2,1,0:T(8,128)}, f32[2,16,32,128]{3,2,1,0:T(8,128)}, u32[]{:S(2)}, u32[]{:S(2)}) collective-permute-start(f32[2,16,32,128]{3,2,1,0:T(8,128)} %pack.48.refs_1_.refs_3_), channel_id=1, source_target_pairs={{0,2},{1,3},{2,0},{3,1},{4,6},{5,7},{6,4},{7,5},{8,10},{9,11},{10,... | collective-permute-start | bytes 1572872 | tf_op jit(solution)/shard_map/ppermute | solution.py:30
  98.3 25.6 %collective-permute-start.17 = (f32[16,32,128]{2,1,0:T(8,128)}, f32[16,32,128]{2,1,0:T(8,128)}, u32[]{:S(2)}, u32[]{:S(2)}) collective-permute-start(f32[16,32,128]{2,1,0:T(8,128)} %get-tuple-element.139), channel_id=1, source_target_pairs={{0,24},{4,28},{8,16},{12,20},{16,8},{20,12},{24,0},{28,4},{1,25},{... | collective-permute-start | bytes 786440 | tf_op jit(solution)/shard_map/ppermute | solution.py:30
  105.7 32.8 %collective-permute-start.21 = (f32[2,16,32,128]{3,2,1,0:T(8,128)}, f32[2,16,32,128]{3,2,1,0:T(8,128)}, u32[]{:S(2)}, u32[]{:S(2)}) collective-permute-start(f32[2,16,32,128]{3,2,1,0:T(8,128)} %pack.50.refs_1_.refs_3_.refs_4_.refs_0_), channel_id=1, source_target_pairs={{0,2},{1,3},{2,0},{3,1},{4,6},{5,7},{6,4},{7,5},{8,10},{9,11},{10,... | collective-permute-start | bytes 1572872 | tf_op jit(solution)/shard_map/ppermute | solution.py:30
  127.9 60.9 %all-gather.15.cloned.1.call-start = ((), (), s32[]{:S(2)}) async-start(), calls=%async_computation.1 | async-start | bytes 1572864 | tf_op jit(solution)/shard_map/all_gather | solution.py:527
  127.9 25.1 %collective-permute-start.23 = (f32[16,32,128]{2,1,0:T(8,128)}, f32[16,32,128]{2,1,0:T(8,128)}, u32[]{:S(2)}, u32[]{:S(2)}) collective-permute-start(f32[16,32,128]{2,1,0:T(8,128)} %get-tuple-element.143), channel_id=1, source_target_pairs={{0,24},{4,28},{8,16},{12,20},{16,8},{20,12},{24,0},{28,4},{1,25},{... | collective-permute-start | bytes 786440 | tf_op jit(solution)/shard_map/ppermute | solution.py:30
  146.6 22.8 %collective-permute-start.27 = (f32[2,16,32,128]{3,2,1,0:T(8,128)}, f32[2,16,32,128]{3,2,1,0:T(8,128)}, u32[]{:S(2)}, u32[]{:S(2)}) collective-permute-start(f32[2,16,32,128]{3,2,1,0:T(8,128)} %pack.55.refs_1_.refs_3_.refs_4_.refs_0_), channel_id=1, source_target_pairs={{0,2},{1,3},{2,0},{3,1},{4,6},{5,7},{6,4},{7,5},{8,10},{9,11},{10,... | collective-permute-start | bytes 1572872 | tf_op jit(solution)/shard_map/ppermute | solution.py:30
  156.8 61.0 %all-gather.13.cloned.1.call-start = ((), (), s32[]{:S(2)}) async-start(), calls=%async_computation | async-start | bytes 1572864 | tf_op jit(solution)/shard_map/all_gather | solution.py:527
  157.1 27.1 %collective-permute-start.29 = (f32[16,32,128]{2,1,0:T(8,128)}, f32[16,32,128]{2,1,0:T(8,128)}, u32[]{:S(2)}, u32[]{:S(2)}) collective-permute-start(f32[16,32,128]{2,1,0:T(8,128)} %get-tuple-element.148), channel_id=1, source_target_pairs={{0,24},{4,28},{8,16},{12,20},{16,8},{20,12},{24,0},{28,4},{1,25},{... | collective-permute-start | bytes 786440 | tf_op jit(solution)/shard_map/ppermute | solution.py:30
  160.2 24.0 %collective-permute-start.30 = (f32[2,16,32,128]{3,2,1,0:T(8,128)}, f32[2,16,32,128]{3,2,1,0:T(8,128)}, u32[]{:S(2)}, u32[]{:S(2)}) collective-permute-start(f32[2,16,32,128]{3,2,1,0:T(8,128)} %pack.57.refs_1_.refs_3_), channel_id=1, source_target_pairs={{0,2},{1,3},{2,0},{3,1},{4,6},{5,7},{6,4},{7,5},{8,10},{9,11},{10,... | collective-permute-start | bytes 1572872 | tf_op jit(solution)/shard_map/ppermute | solution.py:30
  175.7 22.8 %collective-permute-start.33 = (f32[2,16,32,128]{3,2,1,0:T(8,128)}, f32[2,16,32,128]{3,2,1,0:T(8,128)}, u32[]{:S(2)}, u32[]{:S(2)}) collective-permute-start(f32[2,16,32,128]{3,2,1,0:T(8,128)} %pack.60.refs_1_.refs_3_.refs_4_.refs_0_), channel_id=1, source_target_pairs={{0,2},{1,3},{2,0},{3,1},{4,6},{5,7},{6,4},{7,5},{8,10},{9,11},{10,... | collective-permute-start | bytes 1572872 | tf_op jit(solution)/shard_map/ppermute | solution.py:30
  188.0 25.4 %collective-permute-start.35 = (f32[16,32,128]{2,1,0:T(8,128)}, f32[16,32,128]{2,1,0:T(8,128)}, u32[]{:S(2)}, u32[]{:S(2)}) collective-permute-start(f32[16,32,128]{2,1,0:T(8,128)} %get-tuple-element.153), channel_id=1, source_target_pairs={{0,24},{4,28},{8,16},{12,20},{16,8},{20,12},{24,0},{28,4},{1,25},{... | collective-permute-start | bytes 786440 | tf_op jit(solution)/shard_map/ppermute | solution.py:30
  206.8 22.4 %collective-permute-start.39 = (f32[2,16,32,128]{3,2,1,0:T(8,128)}, f32[2,16,32,128]{3,2,1,0:T(8,128)}, u32[]{:S(2)}, u32[]{:S(2)}) collective-permute-start(f32[2,16,32,128]{3,2,1,0:T(8,128)} %pack.65.refs_1_.refs_3_.refs_4_.refs_0_), channel_id=1, source_target_pairs={{0,2},{1,3},{2,0},{3,1},{4,6},{5,7},{6,4},{7,5},{8,10},{9,11},{10,... | collective-permute-start | bytes 1572872 | tf_op jit(solution)/shard_map/ppermute | solution.py:30
  217.1 27.4 %collective-permute-start.41 = (f32[16,32,128]{2,1,0:T(8,128)}, f32[16,32,128]{2,1,0:T(8,128)}, u32[]{:S(2)}, u32[]{:S(2)}) collective-permute-start(f32[16,32,128]{2,1,0:T(8,128)} %get-tuple-element.158), channel_id=1, source_target_pairs={{0,24},{4,28},{8,16},{12,20},{16,8},{20,12},{24,0},{28,4},{1,25},{... | collective-permute-start | bytes 786440 | tf_op jit(solution)/shard_map/ppermute | solution.py:30
  220.1 24.3 %collective-permute-start.42 = (f32[2,16,32,128]{3,2,1,0:T(8,128)}, f32[2,16,32,128]{3,2,1,0:T(8,128)}, u32[]{:S(2)}, u32[]{:S(2)}) collective-permute-start(f32[2,16,32,128]{3,2,1,0:T(8,128)} %pack.67.refs_1_.refs_3_), channel_id=1, source_target_pairs={{0,2},{1,3},{2,0},{3,1},{4,6},{5,7},{6,4},{7,5},{8,10},{9,11},{10,... | collective-permute-start | bytes 1572872 | tf_op jit(solution)/shard_map/ppermute | solution.py:30
  272.3 22.8 %collective-permute-start.53 = (f32[4,2,16,32,128]{4,3,2,1,0:T(8,128)S(1)}, f32[4,2,16,32,128]{4,3,2,1,0:T(8,128)S(1)}, u32[]{:S(2)}, u32[]{:S(2)}) collective-permute-start(f32[4,2,16,32,128]{4,3,2,1,0:T(8,128)S(1)} %pack.77), channel_id=1, source_target_pairs={{0,1},{1,0},{2,3},{3,2},{4,5},{5,4},{6,7},{7,6},{8,9},{9,8},{10,11... | collective-permute-start | bytes 6291464 | tf_op jit(solution)/shard_map/ppermute | solution.py:30
  272.4 29.3 %collective-permute-start.49 = (f32[2,16,32,128]{3,2,1,0:T(8,128)S(1)}, f32[2,16,32,128]{3,2,1,0:T(8,128)S(1)}, u32[]{:S(2)}, u32[]{:S(2)}) collective-permute-start(f32[2,16,32,128]{3,2,1,0:T(8,128)S(1)} %pack.76.refs_4_.refs_1_), channel_id=1, source_target_pairs={{0,2},{1,3},{2,0},{3,1},{4,6},{5,7},{6,4},{7,5},{8,10},{9,11},{10,... | collective-permute-start | bytes 1572872 | tf_op jit(solution)/shard_map/ppermute | solution.py:30
  273.9 28.6 %collective-permute-start.51 = (f32[2,16,32,128]{3,2,1,0:T(8,128)S(1)}, f32[2,16,32,128]{3,2,1,0:T(8,128)S(1)}, u32[]{:S(2)}, u32[]{:S(2)}) collective-permute-start(f32[2,16,32,128]{3,2,1,0:T(8,128)S(1)} %pack.76.refs_4_.refs_1_), channel_id=1, source_target_pairs={{0,1},{1,0},{2,3},{3,2},{4,5},{5,4},{6,7},{7,6},{8,9},{9,8},{10,11... | collective-permute-start | bytes 1572872 | tf_op jit(solution)/shard_map/ppermute | solution.py:30
  (76 other events, 679.5 us)
Sparse Core Ops, SparseCore 0:
  37.1 24.5 all-gather.22
  67.8 21.3 all-gather.20
  94.5 23.8 all-gather.18
  128.0 22.0 all-gather.16
  157.0 22.5 all-gather.14
  188.1 22.0 all-gather.12
